TPU v7x, 256 devices: a whole 4x4x8 slice. The times are simulated.
256 devices in a mesh: section: 2 (over core), tensor: 8 (over z), shard: 16 (over y, x).
Axes of the slice: x: 4, y: 4, z: 8, core: 2. Of those that a mesh axis runs over, the one named last changes fastest.
Arguments:
- embeds: bfloat16 [16, 256, 4096], P('shard', 'tensor'), may hold values from -6 to 6
- segments: int32 [16, 256], P('shard'), may hold values from 0 to 7, never falling along the last dimension, each value on 1 to 64 neighbouring positions
- rel_table: float32 [32, 32], P(None, 'tensor'), may hold values from -320 to 320
- attn_gain: float32 [2, 4096], P('section'), may hold values from 0.25 to 1.75
- w_query: bfloat16 [2, 4096, 2048], P('section', None, 'tensor'), may hold values from -0.01171875 to 0.01171875
- w_key: bfloat16 [2, 4096, 2048], P('section', None, 'tensor'), may hold values from -0.09375 to 0.09375
- w_value: bfloat16 [2, 4096, 2048], P('section', None, 'tensor'), may hold values from -0.09375 to 0.09375
- w_out: bfloat16 [2, 2048, 4096], P('section', 'tensor'), may hold values from -0.125 to 0.125
- ffn_gain: float32 [2, 4096], P('section'), may hold values from 0.25 to 1.75
- w_gate: bfloat16 [2, 4096, 5120], P('section', 'shard', 'tensor'), may hold values from -0.09375 to 0.09375
- w_up: bfloat16 [2, 4096, 5120], P('section', 'shard', 'tensor'), may hold values from -0.09375 to 0.09375
- w_down: bfloat16 [2, 5120, 4096], P('section', 'tensor', 'shard'), may hold values from -0.078125 to 0.078125
- final_gain: float32 [4096], replicated, may hold values from 0.25 to 1.75
- w_proj: bfloat16 [4096, 768], P('tensor'), may hold values from -0.09375 to 0.09375
- dest_shard: int32 [16, 8], P('shard'), may hold values from 0 to 31, as said below
- dest_slot: int32 [16, 8], P('shard'), may hold values from 0 to 3
Outputs:
- index: bfloat16 [128, 768], P(('section', 'shard'))
Inputs may be any that keep to these rules, and one draw needn't show every extreme that they name: `segments`: within a pack the passage number never falls, and each of the 8 passages has 1 to 64 tokens. `dest_shard`: together with dest_slot, each of the 128 index slots receives exactly one passage.
All inputs are finite; a program needn't handle non-finite values.
Results may differ from a plain program's by a relative error of at most 0.033.
Values may be sent and summed in bfloat16 or wider, within the bound.
A program may use at most 128 MiB of HBM per device.

v0:
```python
import jax
import jax.numpy as jnp
from jax import lax
from jax.sharding import PartitionSpec as P

bucket_edges = (12, 16, 23, 32, 46, 64, 91)


def shifted(value, axis, steps):
    count = lax.axis_size(axis)
    initial, last = (max(0, -steps), min(count, count - steps))
    return lax.ppermute(value, axis, [(source, source + steps) for source in range(initial, last)])


def buckets(length):
    position = jnp.arange(length, dtype=jnp.int32)
    relative = position[None, :] - position[:, None]
    forward = (relative > 0).astype(jnp.int32) * 16
    distance = jnp.abs(relative)
    far_code = 8 + sum(((distance >= boundary).astype(jnp.int32) for boundary in bucket_edges))
    return forward + jnp.where(distance < 8, distance, far_code)


def rms_scale(source, norm_gain):
    floats = source.astype(jnp.float32)
    mean_square = jnp.mean(floats * floats, axis=-1, keepdims=True)
    return floats * lax.rsqrt(mean_square + 1e-06) * norm_gain


def attend(normed, seg_full, position_bias, query_rows, key_rows, value_rows, out_rows):
    inner_width = query_rows.shape[1]
    heads_here = position_bias.shape[0]
    head_dim = inner_width // heads_here
    length = normed.shape[0]
    queries = jnp.dot(normed, query_rows, preferred_element_type=jnp.float32).astype(jnp.bfloat16)
    keys_here = jnp.dot(normed, key_rows, preferred_element_type=jnp.float32).astype(jnp.bfloat16)
    values = jnp.dot(normed, value_rows, preferred_element_type=jnp.float32).astype(jnp.bfloat16)
    queries = queries.reshape(length, heads_here, head_dim)
    keys_here = keys_here.reshape(length, heads_here, head_dim)
    values = values.reshape(length, heads_here, head_dim)
    scores = (
        jnp.einsum("qhd,khd->hqk", queries, keys_here, preferred_element_type=jnp.float32)
        + position_bias
    )
    same_passage = seg_full[:, None] == seg_full[None, :]
    scores = jnp.where(same_passage[None], scores, -1e30)
    row_max = jnp.max(scores, axis=-1, keepdims=True)
    weights = jnp.exp(scores - row_max)
    probabilities = (weights / jnp.sum(weights, axis=-1, keepdims=True)).astype(jnp.bfloat16)
    context = jnp.einsum("hqk,khd->qhd", probabilities, values, preferred_element_type=jnp.float32)
    context = context.astype(jnp.bfloat16).reshape(length, inner_width)
    return jnp.dot(context, out_rows, preferred_element_type=jnp.float32)


def on_device(
    embeds,
    segments,
    rel_table,
    attn_gain,
    w_query,
    w_key,
    w_value,
    w_out,
    ffn_gain,
    w_gate,
    w_up,
    w_down,
    final_gain,
    w_proj,
    dest_shard,
    dest_slot,
):
    batches, pack_rows, model_width = embeds.shape
    pack_length = segments.shape[1]
    passages = dest_shard.shape[1]
    sections = lax.axis_size("section")
    section_index = lax.axis_index("section")
    tensor_index = lax.axis_index("tensor")
    slot_count = batches * passages // sections
    bucket_total = rel_table.shape[0]
    bucket_codes = buckets(pack_length).reshape(-1)
    code_table = (
        bucket_codes[:, None] == jnp.arange(bucket_total, dtype=jnp.int32)[None, :]
    ).astype(jnp.float32)
    position_bias = jnp.dot(code_table, rel_table, precision=lax.Precision.HIGHEST).T
    position_bias = position_bias.reshape(rel_table.shape[1], pack_length, pack_length)
    query_rows, key_rows, value_rows, out_rows = (w_query[0], w_key[0], w_value[0], w_out[0])
    attn_scale, ffn_scale = (attn_gain[0], ffn_gain[0])
    full_gate, full_up, full_down = (
        lax.all_gather(w_gate[0], "shard", axis=0, tiled=True),
        lax.all_gather(w_up[0], "shard", axis=0, tiled=True),
        lax.all_gather(w_down[0], "shard", axis=1, tiled=True),
    )

    def feed(normed):
        gate_part = jnp.dot(normed, full_gate, preferred_element_type=jnp.float32)
        up_part = jnp.dot(normed, full_up, preferred_element_type=jnp.float32)
        activation = (jax.nn.gelu(gate_part, approximate=True) * up_part).astype(jnp.bfloat16)
        return jnp.dot(activation, full_down, preferred_element_type=jnp.float32)

    def total_rows_sum(partial_value):
        return lax.psum(partial_value.astype(jnp.bfloat16), "tensor").astype(jnp.float32)

    def run_layer(rows_in, seg_full):
        whole_rows = lax.all_gather(rows_in, "tensor", axis=0, tiled=True)
        normed = rms_scale(whole_rows, attn_scale).astype(jnp.bfloat16)
        attended = total_rows_sum(
            attend(normed, seg_full, position_bias, query_rows, key_rows, value_rows, out_rows)
        )
        middle = (whole_rows.astype(jnp.float32) + attended).astype(jnp.bfloat16)
        normed2 = rms_scale(middle, ffn_scale).astype(jnp.bfloat16)
        fed = total_rows_sum(feed(normed2))
        finished_rows = (middle.astype(jnp.float32) + fed).astype(jnp.bfloat16)
        return lax.dynamic_slice_in_dim(finished_rows, tensor_index * pack_rows, pack_rows, 0)

    def advance(step_index, carry):
        incoming, pooled = carry
        pack_index = step_index - section_index
        active = (pack_index >= 0) & (pack_index < batches)
        chosen = jnp.clip(pack_index, 0, batches - 1)
        fresh = lax.dynamic_index_in_dim(embeds, chosen, 0, keepdims=False)
        rows_in = jnp.where(section_index == 0, fresh, incoming)
        seg_full = lax.dynamic_index_in_dim(segments, chosen, 0, keepdims=False)
        computed = run_layer(rows_in, seg_full)
        rows_out = jnp.where(active, computed, rows_in)
        finished = rms_scale(rows_out, final_gain)
        seg_rows = lax.dynamic_slice_in_dim(seg_full, tensor_index * pack_rows, pack_rows)
        member = (jnp.arange(passages, dtype=jnp.int32)[:, None] == seg_rows[None, :]).astype(
            jnp.float32
        )
        passage_sums = jnp.dot(member, finished, precision=lax.Precision.HIGHEST)
        wanted = active & (section_index == sections - 1)
        current = lax.dynamic_index_in_dim(pooled, chosen, 0, keepdims=False)
        updated = jnp.where(wanted, current + passage_sums, current)
        pooled = lax.dynamic_update_index_in_dim(pooled, updated, chosen, 0)
        return (shifted(rows_out, "section", 1), pooled)

    start_rows = jnp.zeros((pack_rows, model_width), jnp.bfloat16)
    start_pooled = jnp.zeros((batches, passages, model_width), jnp.float32)
    last_rows, pooled = lax.fori_loop(
        0, batches + sections - 1, advance, (start_rows, start_pooled)
    )
    pooled_cols = lax.psum_scatter(
        pooled.reshape(batches * passages, model_width).astype(jnp.bfloat16),
        "tensor",
        scatter_dimension=1,
        tiled=True,
    ).astype(jnp.float32)
    member_all = (
        segments[:, :, None] == jnp.arange(passages, dtype=jnp.int32)[None, None, :]
    ).astype(jnp.float32)
    counts = jnp.sum(member_all, axis=1).reshape(batches * passages, 1)
    means = (pooled_cols / counts).astype(jnp.bfloat16)
    projected_cols = lax.psum_scatter(
        jnp.dot(means, w_proj, preferred_element_type=jnp.float32),
        "tensor",
        scatter_dimension=1,
        tiled=True,
    )
    projected = lax.all_gather(projected_cols, "tensor", axis=1, tiled=True)
    unit = projected * lax.rsqrt(jnp.mean(projected * projected, axis=-1, keepdims=True) + 1e-06)
    unit = jnp.where(section_index == sections - 1, unit, 0.0)
    target = (dest_shard * slot_count + dest_slot).reshape(-1)
    total_rows = sections * lax.axis_size("shard") * slot_count
    placing = (jnp.arange(total_rows, dtype=jnp.int32)[:, None] == target[None, :]).astype(
        jnp.float32
    )
    placed = jnp.dot(placing, unit, precision=lax.Precision.HIGHEST)
    return lax.psum_scatter(
        placed.astype(jnp.bfloat16), ("section", "shard"), scatter_dimension=0, tiled=True
    )


def solution(mesh):
    in_specs = (
        P("shard", "tensor", None),
        P("shard", None),
        P(None, "tensor"),
        P("section", None),
        P("section", None, "tensor"),
        P("section", None, "tensor"),
        P("section", None, "tensor"),
        P("section", "tensor", None),
        P("section", None),
        P("section", "shard", "tensor"),
        P("section", "shard", "tensor"),
        P("section", "tensor", "shard"),
        P(),
        P("tensor", None),
        P("shard", None),
        P("shard", None),
    )
    out_specs = P(("section", "shard"), None)
    return jax.shard_map(
        on_device, mesh=mesh, in_specs=in_specs, out_specs=out_specs, check_vma=False
    )
```

profile of v0, /device:TPU:1, one launch (start us, length us, event | category | flops | bytes accessed | tf_op | source)
XLA Modules:
  0.0 914.7 jit_solution(18233234397185593786)
XLA Ops:
  9.3 2.6 fusion.43
  12.2 1.4 copy.26
  14.2 60.9 %all-gather.9.cloned.1.call-done = bf16[1,4096,640]{2,1,0:T(8,128)(2,1)} async-done(((bf16[1,256,640]{2,1,0:T(8,128)(2,1)}), bf16[1,4096,640]{2,1,0:T(8,128)(2,1)}) %all-gather.9.cloned.1.call-update) | async-done | bytes 5242896 | tf_op jit(solution)/shard_map/all_gather | solution.py:90
  75.0 63.6 %all-gather.11.cloned.1.call-done = bf16[1,4096,640]{2,1,0:T(8,128)(2,1)} async-done(((bf16[1,256,640]{2,1,0:T(8,128)(2,1)}), bf16[1,4096,640]{2,1,0:T(8,128)(2,1)}) %all-gather.11.cloned.1.call-update) | async-done | bytes 5242896 | tf_op jit(solution)/shard_map/all_gather | solution.py:91
  138.6 69.0 %all-gather.13.cloned.1.call-done = bf16[1,640,4096]{2,1,0:T(8,128)(2,1)} async-done(((bf16[1,640,256]{2,1,0:T(8,128)(2,1)}), bf16[1,640,4096]{2,1,0:T(8,128)(2,1)}) %all-gather.13.cloned.1.call-update) | async-done | bytes 5242896 | tf_op jit(solution)/shard_map/all_gather | solution.py:92
  207.7 488.1 %while.17 = (s32[]{:T(128)}, bf16[32,4096]{1,0:T(8,128)(2,1)S(1)}, f32[1,8,4096]{2,1,0:T(8,128)S(1)}, s32[]{:T(128)}, pred[]{:T(512)}, /*index=5*/bf16[1,32,4096...) while((s32[]{:T(128)}, bf16[32,4096]{1,0:T(8,128)(2,1)S(1)}, ...), condition=%wide.region_8.9_spmd, body=%wide.region_0.8_spmd.sunk | while | flops 6303057920 | bytes 139323248 | solution.py:140
  207.9 0.8 bitcast_select_fusion.2
  208.9 39.2 %all-gather.15.cloned.1.call-done = bf16[256,4096]{1,0:T(8,128)(2,1)} async-done(((bf16[32,4096]{1,0:T(8,128)(2,1)}), bf16[256,4096]{1,0:T(8,128)(2,1)}) %all-gather.15.cloned.1.call-update) | async-done | bytes 2097168 | tf_op jit(solution)/shard_map/while/body/eval_jaxpr/all_gather | solution.py:105
  248.1 2.2 fusion.113
  250.4 2.9 convolution_convert_fusion.15
  253.3 1.2 convolution_convert_fusion.14
  254.9 1.0 copy-done.2
  256.5 1.9 convolution_convert_fusion.13
  258.3 2.0 convolution_convert_fusion.16
  260.3 3.6 convolution_convert_fusion.17
  264.0 81.2 %all-reduce.7.cloned.1.call-done = bf16[256,4096]{1,0:T(8,128)(2,1)} async-done(((bf16[256,4096]{1,0:T(8,128)(2,1)}), bf16[256,4096]{1,0:T(8,128)(2,1)}) %all-reduce.7.cloned.1.call-update) | async-done | bytes 2097168 | tf_op jit(solution)/shard_map/while/body/eval_jaxpr/psum | solution.py:102
  345.2 4.4 fusion.116
  349.5 5.2 fusion.117
  354.8 9.7 %convolution_convert_fusion.18 = bf16[256,4096]{1,0:T(8,128)(2,1)} fusion(bf16[640,4096]{1,0:T(8,128)(2,1)} %get-tuple-element.754, bf16[4096,640]{1,0:T(8,128)(2,1)} %get-tuple-element.753, f32[256,640]{1,0:T(8,128)} %fusion.117, f32[4096]{0:T(1024)S(1)} %bitcast.134, f32[256]{0:T(256)S(1)} %add_rsqrt_fusion.8, ...), kind=kOutput, calls=%fused_computation.4.clone.1 | convolution fusion | flops 2695430144 | bytes 17449984 | tf_op jit(solution)/shard_map/while/body/eval_jaxpr/dot_general | solution.py:99
  364.5 80.9 %all-reduce.9.cloned.1.call-done = bf16[256,4096]{1,0:T(8,128)(2,1)} async-done(((bf16[256,4096]{1,0:T(8,128)(2,1)}), bf16[256,4096]{1,0:T(8,128)(2,1)}) %all-reduce.9.cloned.1.call-update) | async-done | bytes 2097168 | tf_op jit(solution)/shard_map/while/body/eval_jaxpr/psum | solution.py:102
  445.3 1.3 fusion.118
  446.7 1.3 collective-permute-start
  448.4 4.2 collective-permute-done
  452.7 0.8 bitcast_select_fusion.2
  453.6 37.5 %all-gather.15.cloned.1.call-done = bf16[256,4096]{1,0:T(8,128)(2,1)} async-done(((bf16[32,4096]{1,0:T(8,128)(2,1)}), bf16[256,4096]{1,0:T(8,128)(2,1)}) %all-gather.15.cloned.1.call-update) | async-done | bytes 2097168 | tf_op jit(solution)/shard_map/while/body/eval_jaxpr/all_gather | solution.py:105
  491.2 2.2 fusion.113
  493.4 2.9 convolution_convert_fusion.15
  496.4 1.2 convolution_convert_fusion.14
  498.0 1.0 copy-done.2
  499.5 1.9 convolution_convert_fusion.13
  501.4 2.0 convolution_convert_fusion.16
  503.3 3.6 convolution_convert_fusion.17
  507.1 81.2 %all-reduce.7.cloned.1.call-done = bf16[256,4096]{1,0:T(8,128)(2,1)} async-done(((bf16[256,4096]{1,0:T(8,128)(2,1)}), bf16[256,4096]{1,0:T(8,128)(2,1)}) %all-reduce.7.cloned.1.call-update) | async-done | bytes 2097168 | tf_op jit(solution)/shard_map/while/body/eval_jaxpr/psum | solution.py:102
  588.2 4.4 fusion.116
  592.6 5.2 fusion.117
  597.9 9.7 %convolution_convert_fusion.18 = bf16[256,4096]{1,0:T(8,128)(2,1)} fusion(bf16[640,4096]{1,0:T(8,128)(2,1)} %get-tuple-element.754, bf16[4096,640]{1,0:T(8,128)(2,1)} %get-tuple-element.753, f32[256,640]{1,0:T(8,128)} %fusion.117, f32[4096]{0:T(1024)S(1)} %bitcast.134, f32[256]{0:T(256)S(1)} %add_rsqrt_fusion.8, ...), kind=kOutput, calls=%fused_computation.4.clone.1 | convolution fusion | flops 2695430144 | bytes 17449984 | tf_op jit(solution)/shard_map/while/body/eval_jaxpr/dot_general | solution.py:99
  607.6 80.9 %all-reduce.9.cloned.1.call-done = bf16[256,4096]{1,0:T(8,128)(2,1)} async-done(((bf16[256,4096]{1,0:T(8,128)(2,1)}), bf16[256,4096]{1,0:T(8,128)(2,1)}) %all-reduce.9.cloned.1.call-update) | async-done | bytes 2097168 | tf_op jit(solution)/shard_map/while/body/eval_jaxpr/psum | solution.py:102
  688.4 1.3 fusion.118
  689.8 1.3 collective-permute-start
  691.5 4.2 collective-permute-done
  696.6 31.5 %reduce-scatter.5.cloned.1.call-done = bf16[8,512]{1,0:T(8,128)(2,1)} async-done(((bf16[8,4096]{1,0:T(8,128)(2,1)}), bf16[8,512]{1,0:T(8,128)(2,1)}) %reduce-scatter.5.cloned.1.call-update) | async-done | bytes 8208 | tf_op jit(solution)/shard_map/reduce_scatter | solution.py:143
  728.1 1.9 convolution_bitcast_fusion
  730.8 36.1 %reduce-scatter.7.cloned.1.call-done = f32[96,8]{1,0:T(8,128)} async-done(((f32[768,8]{1,0:T(8,128)}), f32[96,8]{1,0:T(8,128)}) %reduce-scatter.7.cloned.1.call-update) | async-done | bytes 3088
  766.9 0.9 copy.30
  767.7 18.1 %all-gather.3 = f32[8,96,8]{1,2,0:T(8,128)S(1)} all-gather(f32[1,96,8]{1,2,0:T(8,128)S(1)} %bitcast.122), channel_id=1, replica_groups=mesh['section'=2,'tensor'=8,'shard'=16] {'tensor'}, dimensions={0}, use_global_device_ids=true | all-gather | bytes 27648 | tf_op jit(solution)/shard_map/all_gather | solution.py:160
  786.1 1.0 convolution_convert_fusion.6
  788.4 118.1 %all-reduce.5.cloned.1.call-done = bf16[128,768]{1,0:T(8,128)(2,1)} async-done(((bf16[128,768]{1,0:T(8,128)(2,1)}), bf16[128,768]{1,0:T(8,128)(2,1)}) %all-reduce.5.cloned.1.call-update) | async-done | bytes 196624
  906.5 1.3 constant_dynamic-slice_fusion
  (111 shorter events, 9.3 us)
Async XLA Ops:
  6.5 721.5 %copy-start = (bf16[512,768]{1,0:T(8,128)(2,1)S(1)}, bf16[512,768]{1,0:T(8,128)(2,1)}, u32[]{:S(2)}) copy-start(bf16[512,768]{1,0:T(8,128)(2,1)} %param.31) | copy-start | bytes 2359300
  6.5 2.8 copy-start.16
  6.5 68.5 %all-gather.9.cloned.1.call-start = ((), (), s32[]{:S(2)}) async-start(), calls=%async_computation.3 | async-start | bytes 5570560 | tf_op jit(solution)/shard_map/all_gather | solution.py:90
  7.3 131.4 %all-gather.11.cloned.1.call-start = ((), (), s32[]{:S(2)}) async-start(), calls=%async_computation.4 | async-start | bytes 5570560 | tf_op jit(solution)/shard_map/all_gather | solution.py:91
  8.0 199.6 %all-gather.13.cloned.1.call-start = ((), (), s32[]{:S(2)}) async-start(), calls=%async_computation.5 | async-start | bytes 5570560 | tf_op jit(solution)/shard_map/all_gather | solution.py:92
  12.0 1.6 copy-start.8
  12.0 195.7 %copy-start.6 = (bf16[1,32,4096]{2,1,0:T(8,128)(2,1)S(1)}, bf16[1,32,4096]{2,1,0:T(8,128)(2,1)}, u32[]{:S(2)}) copy-start(bf16[1,32,4096]{2,1,0:T(8,128)(2,1)} %param.18) | copy-start | bytes 786436
  12.0 195.7 %copy-start.7 = (f32[4096]{0:T(1024)S(1)}, f32[4096]{0:T(1024)}, u32[]{:S(2)}) copy-start(f32[4096]{0:T(1024)} %param.30) | copy-start | bytes 49156
  12.2 195.5 %copy-start.9 = (s32[1,256]{1,0:T(1,128)S(1)}, s32[1,256]{1,0:T(1,128)}, u32[]{:S(2)}) copy-start(s32[1,256]{1,0:T(1,128)} %param.19) | copy-start | bytes 3076
  207.9 40.2 %all-gather.15.cloned.1.call-start = ((), (), s32[]{:S(2)}) async-start(), calls=%async_computation.8 | async-start | bytes 2359296 | tf_op jit(solution)/shard_map/while/body/eval_jaxpr/all_gather | solution.py:105
  208.7 41.6 %copy-start.14 = (f32[1,4096]{1,0:T(1,128)S(1)}, f32[1,4096]{1,0:T(1,128)}, u32[]{:S(2)}) copy-start(f32[1,4096]{1,0:T(1,128)} %get-tuple-element.744) | copy-start | bytes 49156 | tf_op jit(solution)/shard_map/while
  208.7 136.4 %all-reduce.7.cloned.1.call-start = ((), (), s32[]{:S(2)}) async-start(), calls=%async_computation.9 | async-start | bytes 4194304 | tf_op jit(solution)/shard_map/while/body/eval_jaxpr/psum | solution.py:102
  248.1 2.3 copy-start.1
  250.3 2.9 copy-start.13
  253.3 1.2 copy-start.5
  254.5 2.0 copy-start.12
  254.9 1.0 copy-start.2
  263.9 85.6 %copy-start.15 = (f32[1,4096]{1,0:T(1,128)S(1)}, f32[1,4096]{1,0:T(1,128)}, u32[]{:S(2)}) copy-start(f32[1,4096]{1,0:T(1,128)} %get-tuple-element.751) | copy-start | bytes 49156 | tf_op jit(solution)/shard_map/while
  263.9 181.4 %all-reduce.9.cloned.1.call-start = ((), (), s32[]{:S(2)}) async-start(), calls=%async_computation.10 | async-start | bytes 4194304 | tf_op jit(solution)/shard_map/while/body/eval_jaxpr/psum | solution.py:102
  345.2 4.4 copy-start.4
  364.4 80.9 %copy-start.3 = (bf16[32,4096]{1,0:T(8,128)(2,1)S(1)}, bf16[32,4096]{1,0:T(8,128)(2,1)}, u32[]{:S(2)}) copy-start(bf16[32,4096]{1,0:T(8,128)(2,1)} %bitcast_select_fusion.2) | copy-start | bytes 786436 | tf_op jit(solution)/shard_map/while
  364.4 83.6 %copy-start.11 = (s32[1,32]{1,0:T(1,128)S(1)}, s32[1,32]{1,0:T(1,128)}, u32[]{:S(2)}) copy-start(s32[1,32]{1,0:T(1,128)} %get-tuple-element.757) | copy-start | bytes 388 | tf_op jit(solution)/shard_map/while
  364.4 88.2 %copy-start.10 = (s32[1,256]{1,0:T(1,128)S(1)}, s32[1,256]{1,0:T(1,128)}, u32[]{:S(2)}) copy-start(s32[1,256]{1,0:T(1,128)} %get-tuple-element.816) | copy-start | bytes 3076 | tf_op jit(solution)/shard_map/while
  446.7 6.0 collective-permute-start
  452.7 38.5 %all-gather.15.cloned.1.call-start = ((), (), s32[]{:S(2)}) async-start(), calls=%async_computation.8 | async-start | bytes 2359296 | tf_op jit(solution)/shard_map/while/body/eval_jaxpr/all_gather | solution.py:105
  453.4 40.0 %copy-start.14 = (f32[1,4096]{1,0:T(1,128)S(1)}, f32[1,4096]{1,0:T(1,128)}, u32[]{:S(2)}) copy-start(f32[1,4096]{1,0:T(1,128)} %get-tuple-element.744) | copy-start | bytes 49156 | tf_op jit(solution)/shard_map/while
  453.5 134.8 %all-reduce.7.cloned.1.call-start = ((), (), s32[]{:S(2)}) async-start(), calls=%async_computation.9 | async-start | bytes 4194304 | tf_op jit(solution)/shard_map/while/body/eval_jaxpr/psum | solution.py:102
  491.2 2.3 copy-start.1
  493.4 2.9 copy-start.13
  496.4 1.2 copy-start.5
  497.6 2.0 copy-start.12
  497.9 1.0 copy-start.2
  507.0 85.6 %copy-start.15 = (f32[1,4096]{1,0:T(1,128)S(1)}, f32[1,4096]{1,0:T(1,128)}, u32[]{:S(2)}) copy-start(f32[1,4096]{1,0:T(1,128)} %get-tuple-element.751) | copy-start | bytes 49156 | tf_op jit(solution)/shard_map/while
  507.0 181.4 %all-reduce.9.cloned.1.call-start = ((), (), s32[]{:S(2)}) async-start(), calls=%async_computation.10 | async-start | bytes 4194304 | tf_op jit(solution)/shard_map/while/body/eval_jaxpr/psum | solution.py:102
  588.2 4.4 copy-start.4
  607.5 80.9 %copy-start.3 = (bf16[32,4096]{1,0:T(8,128)(2,1)S(1)}, bf16[32,4096]{1,0:T(8,128)(2,1)}, u32[]{:S(2)}) copy-start(bf16[32,4096]{1,0:T(8,128)(2,1)} %bitcast_select_fusion.2) | copy-start | bytes 786436 | tf_op jit(solution)/shard_map/while
  607.5 83.6 %copy-start.11 = (s32[1,32]{1,0:T(1,128)S(1)}, s32[1,32]{1,0:T(1,128)}, u32[]{:S(2)}) copy-start(s32[1,32]{1,0:T(1,128)} %get-tuple-element.757) | copy-start | bytes 388 | tf_op jit(solution)/shard_map/while
  607.5 88.2 %copy-start.10 = (s32[1,256]{1,0:T(1,128)S(1)}, s32[1,256]{1,0:T(1,128)}, u32[]{:S(2)}) copy-start(s32[1,256]{1,0:T(1,128)} %get-tuple-element.816) | copy-start | bytes 3076 | tf_op jit(solution)/shard_map/while
  689.8 6.0 collective-permute-start
  695.8 91.4 %copy-start.17 = (u32[256]{0:T(256)S(1)}, u32[256]{0:T(256)}, u32[]{:S(2)}) copy-start(u32[256]{0:T(256)} %constant.205) | copy-start | bytes 3076
  695.8 32.3 %reduce-scatter.5.cloned.1.call-start = ((), (), s32[]{:S(2)}) async-start(), calls=%async_computation.2 | async-start | bytes 73728 | tf_op jit(solution)/shard_map/reduce_scatter | solution.py:143
  696.4 70.5 %reduce-scatter.7.cloned.1.call-start = ((), (), s32[]{:S(2)}) async-start(), calls=%async_computation.6 | async-start | bytes 442368
  730.0 176.5 %all-reduce.5.cloned.1.call-start = ((), (), s32[]{:S(2)}) async-start(), calls=%async_computation.7 | async-start | bytes 393216
Sparse Core Ops, SparseCore 0:
  9.8 65.1 all-gather.8
  77.5 61.1 all-gather.10
  141.0 66.5 all-gather.12
  210.3 37.7 all-gather.14
  264.0 81.0 all-reduce.6
  364.6 80.7 all-reduce.8
  455.4 35.7 all-gather.14
  507.1 81.0 all-reduce.6
  607.7 80.7 all-reduce.8
  698.8 29.2 reduce-scatter.4
  730.8 36.0 reduce-scatter.6
  787.3 119.2 all-reduce.4
where the time goes:
time: 915 us
  waiting for transfers between devices  791 us (86%)
  matrix products  60 us (7%)
  other arithmetic  19.9 us (2%)
  blocking collectives  18.1 us (2%)
  between operations  14.3 us (2%)
    psum x4, waiting for transfers between devices, total_rows_sum(): lax.psum(partial_value.astype(jnp.bfloat16), 'tensor').astype(jnp.float32)  324 us
    unnamed x8, waiting for transfers between devices  156 us
    all_gather x2, waiting for transfers between devices, run_layer(): whole_rows = lax.all_gather(rows_in, 'tensor', axis=0, tiled=True)  76.8 us
    all_gather x1, waiting for transfers between devices, on_device(): lax.all_gather(w_down[0], 'shard', axis=1, tiled=True)  69 us
    all_gather x1, waiting for transfers between devices, on_device(): lax.all_gather(w_up[0], 'shard', axis=0, tiled=True)  63.6 us
    all_gather x1, waiting for transfers between devices, on_device(): lax.all_gather(w_gate[0], 'shard', axis=0, tiled=True)  60.9 us
    reduce_scatter x1, waiting for transfers between devices, on_device(): lax.psum_scatter(pooled.reshape(batches * passages, model_width).astype(j...  31.5 us
    dot_general x2, matrix products, feed(): return jnp.dot(activation, full_down, preferred_element_type=jnp.float32)  19.3 us
  transfers between devices with their start and end apart: 14, of which 14 were waited for; matrix products, arithmetic and copies ran while one was open for 1% of the time, Pallas kernels for 0%

commit v1 on v0

v1 whole, which is shorter than its diff:
```python
import functools

import jax
import jax.numpy as jnp
from jax import lax
from jax.experimental import pallas as pl
from jax.experimental.pallas import tpu as pltpu
from jax.sharding import PartitionSpec as P

MESH = pl.DeviceIdType.MESH
F32 = jnp.float32
BF16 = jnp.bfloat16
HIGHEST = lax.Precision.HIGHEST

ROWS = 32
CHUNK = 16
RINGZ = 8
SIDE = 4
SHARDS = SIDE * SIDE
WIDTH = 4096
SEQ = 256
HEADS = 4
PPM = 8
DK = 256
HID = 640
EMB = 768
HALF = EMB // 2
PCOLS = WIDTH // RINGZ
EPS = 1e-06

lowest = (0, 1, 2, 3, 4, 5, 6, 7, 8, 12, 16, 23, 32, 46, 64, 91)


def copy_to(src, dst, send, recv, device):
    return pltpu.make_async_remote_copy(
        src_ref=src,
        dst_ref=dst,
        send_sem=send,
        recv_sem=recv,
        device_id=device,
        device_id_type=MESH,
    )


def normed(rows, gain):
    mean_square = jnp.mean(rows * rows, axis=-1, keepdims=True)
    return rows * lax.rsqrt(mean_square + EPS) * gain


def gather_rows(z, blocks, send, recv):
    right, left = lax.rem(z + 1, RINGZ), lax.rem(z + RINGZ - 1, RINGZ)

    def going(way, step, c):
        back = step - 1
        owner = lax.rem(z + RINGZ - back, RINGZ) if way == 0 else lax.rem(z + back, RINGZ)
        at = (way * 4 + step - 1) * 2 + c
        ref = blocks.at[2 * owner + c]
        return copy_to(ref, ref, send.at[at], recv.at[at], {"tensor": right if way == 0 else left})

    def coming(way, step, c):
        owner = lax.rem(z + RINGZ - step, RINGZ) if way == 0 else lax.rem(z + step, RINGZ)
        at = (way * 4 + step - 1) * 2 + c
        ref = blocks.at[2 * owner + c]
        return copy_to(ref, ref, send.at[at], recv.at[at], {"tensor": right if way == 0 else left})

    sent = []
    for step in (1, 2, 3):
        for c in (0, 1):
            for way in (0, 1):
                if step > 1:
                    coming(way, step - 1, c).wait_recv()
                moving = going(way, step, c)
                moving.start()
                sent.append(moving)
    for way in (0, 1):
        coming(way, 3, way).wait_recv()
        moving = going(way, 4, way)
        moving.start()
        sent.append(moving)
    for way in (0, 1):
        coming(way, 3, 1 - way).wait_recv()
    for way in (0, 1):
        coming(way, 4, way).wait_recv()
    return sent


def sum_rows(z, parts, landed, send, recv):
    right, left = lax.rem(z + 1, RINGZ), lax.rem(z + RINGZ - 1, RINGZ)

    def place(way, step, c):
        return way * 8 + (step - 1) * 2 + c

    def going(way, step, c):
        ahead = 5 - step
        owner = lax.rem(z + ahead, RINGZ) if way == 0 else lax.rem(z + RINGZ - ahead, RINGZ)
        at = place(way, step, c)
        index = 2 * owner + c
        return index, copy_to(
            parts.at[index],
            landed.at[at],
            send.at[at],
            recv.at[at],
            {"tensor": right if way == 0 else left},
        )

    def arrived(way, step, c):
        going(way, step, c)[1].wait_recv()
        return landed[place(way, step, c)].astype(F32)

    sent = []

    def forward(way, step, c, adds):
        index, moving = going(way, step, c)
        if adds:
            total = parts[index].astype(F32) + arrived(way, step - 1, c)
            parts[index] = total.astype(BF16)
        moving.start()
        sent.append(moving)

    for way in (0, 1):
        forward(way, 1, way, False)
    for way in (0, 1):
        forward(way, 2, 1 - way, False)
    for way in (0, 1):
        forward(way, 2, way, True)
    for step in (3, 4):
        for first in (1, 0):
            for way in (0, 1):
                forward(way, step, way if first == 0 else 1 - way, True)

    def total(c):
        own = parts[2 * z + c].astype(F32)
        return own + arrived(0, 4, c) + arrived(1, 4, c)

    return sent, total


def gather_weights(y, x, gate, up, down, send, recv):
    def neighbour(axis, sign):
        step = 1 if sign == 0 else SIDE - 1
        if axis == 0:
            return {"shard": y * SIDE + lax.rem(x + step, SIDE)}
        return {"shard": lax.rem(y + step, SIDE) * SIDE + x}

    def behind(axis, sign):
        step = SIDE - 1 if sign == 0 else 1
        return lax.rem((x if axis == 0 else y) + step, SIDE)

    halves = {0: (0, DK // 2), 1: (DK // 2, DK // 2)}
    part = HID // 2
    quarter = HID // 4

    def pieces(array, at_y, at_x, sign):
        if array == 0:
            lead = gate.at[at_y] if at_x is None else gate.at[at_y, at_x]
            start, size = (0, DK) if sign is None else halves[sign]
        elif array == 1:
            lead = up.at[:, at_x] if at_y is None else up.at[at_y, at_x]
            start, size = (0, DK) if sign is None else halves[sign]
        else:
            if at_x is None:
                lead = down.at[at_y]
            elif at_y is None:
                lead = down.at[:, at_x]
            else:
                lead = down.at[at_y, at_x]
            base = 0 if array == 2 else part
            start, size = (base, part) if sign is None else (base + sign * quarter, quarter)
        rows = pl.ds(start, size)
        return lead.at[rows] if at_x is not None and at_y is not None else lead.at[:, rows]

    sent = []
    first_axis = {0: 0, 2: 0, 1: 1, 3: 1}

    def where(array, axis, coordinate, stage):
        if axis == 0:
            return (y if stage == 0 else None, coordinate)
        return (coordinate, x if stage == 0 else None)

    def move(stage, hop, array, sign):
        axis = first_axis[array] if stage == 0 else 1 - first_axis[array]
        at = ((stage * 2 + hop) * 4 + array) * 2 + sign
        own = x if axis == 0 else y
        coordinate = own if hop == 0 else behind(axis, sign)
        ref = pieces(array, *where(array, axis, coordinate, stage), None if hop == 0 else sign)
        return copy_to(ref, ref, send.at[at], recv.at[at], neighbour(axis, sign))

    def landing(stage, hop, array, sign):
        axis = first_axis[array] if stage == 0 else 1 - first_axis[array]
        at = ((stage * 2 + hop) * 4 + array) * 2 + sign
        own = x if axis == 0 else y
        coordinate = behind(axis, sign) if hop == 0 else lax.rem(own + 2, SIDE)
        ref = pieces(array, *where(array, axis, coordinate, stage), None if hop == 0 else sign)
        return copy_to(ref, ref, send.at[at], recv.at[at], neighbour(axis, sign))

    for stage in (0, 1):
        for hop in (0, 1):
            for array in range(4):
                for sign in (0, 1):
                    if hop == 1:
                        landing(stage, 0, array, sign).wait_recv()
                    moving = move(stage, hop, array, sign)
                    moving.start()
                    sent.append(moving)
        for array in range(4):
            for sign in (0, 1):
                landing(stage, 1, array, sign).wait_recv()
    for moving in sent:
        moving.wait_send()


def kernel(
    embeds,
    segments,
    segments_s,
    rel_s,
    attn_gain,
    w_query,
    w_key,
    w_value,
    w_out,
    ffn_gain,
    w_gate,
    w_up,
    w_down,
    final_gain,
    w_proj,
    dest_shard,
    dest_slot,
    index,
    query_w,
    key_w,
    value_w,
    out_w,
    proj_w,
    gate_w,
    up_w,
    down_w,
    bias,
    member_here,
    attn_rows,
    attn_parts,
    attn_landed,
    ffn_rows,
    ffn_parts,
    ffn_landed,
    attn_in,
    handed,
    ffn_in,
    gain_in,
    queries,
    keys,
    values,
    context,
    sums,
    hidden,
    pooled,
    pooled_in,
    shares,
    placed,
    placed_in,
    load_sem,
    swap_send,
    swap_recv,
    hand_send,
    hand_recv,
    ag_send,
    ag_recv,
    rs_send,
    rs_recv,
    w_send,
    w_recv,
    pool_send,
    pool_recv,
    share_send,
    share_recv,
    place_send,
    place_recv,
):
    section = lax.axis_index("section")
    z = lax.axis_index("tensor")
    shard = lax.axis_index("shard")
    y, x = shard // SIDE, lax.rem(shard, SIDE)
    other = 1 - section

    barrier = pltpu.get_barrier_semaphore()

    def greet(device):
        pl.semaphore_signal(barrier, inc=1, device_id=device, device_id_type=MESH)

    @pl.loop(1, RINGZ)
    def _(k):
        greet({"tensor": lax.rem(z + k, RINGZ)})

    @pl.loop(1, SHARDS)
    def _(k):
        greet({"shard": lax.rem(shard + k, SHARDS)})

    @pl.loop(0, SHARDS)
    def _(k):
        greet({"section": other, "shard": lax.rem(shard + k, SHARDS)})

    loads = [
        pltpu.make_async_copy(src, dst, load_sem.at[i])
        for i, (src, dst) in enumerate(
            (
                (w_query.at[0], query_w),
                (w_key.at[0], key_w),
                (w_value.at[0], value_w),
                (w_out.at[0], out_w),
                (w_proj, proj_w),
            )
        )
    ]
    for load in loads:
        load.start()

    passage = lax.broadcasted_iota(jnp.int32, (PPM, SEQ), 0)
    member = (passage == segments[...]).astype(F32)
    same = lax.dot_general(
        member.astype(BF16),
        member.astype(BF16),
        (((0,), (0,)), ((), ())),
        preferred_element_type=F32,
    )
    counts = jnp.sum(member, axis=-1, keepdims=True)
    bias[0] = same

    here_row = lax.broadcasted_iota(jnp.int32, (PPM, ROWS), 0)
    here_col = lax.broadcasted_iota(jnp.int32, (PPM, ROWS), 1)
    here = jnp.zeros((PPM, ROWS), F32)
    for r in range(ROWS):
        here = jnp.where((here_col == r) & (here_row == segments_s[0, z * ROWS + r]), 1.0, here)
    member_here[...] = here

    @pl.loop(0, SEQ // ROWS)
    def _(block):
        rows = pl.ds(pl.multiple_of(block * ROWS, ROWS), ROWS)
        inside = bias[0, rows, :] > 0.5
        i = lax.broadcasted_iota(jnp.int32, (ROWS, SEQ), 0) + block * ROWS
        k = lax.broadcasted_iota(jnp.int32, (ROWS, SEQ), 1)
        ahead = k - i
        distance = jnp.abs(ahead)
        for head in range(HEADS):
            before = jnp.full((ROWS, SEQ), rel_s[0, head], F32)
            after = jnp.full((ROWS, SEQ), rel_s[16, head], F32)
            for code in range(1, 16):
                reached = distance >= lowest[code]
                before = jnp.where(reached, rel_s[code, head], before)
                after = jnp.where(reached, rel_s[16 + code, head], after)
            value = jnp.where(ahead > 0, after, before)
            bias[head, rows, :] = jnp.where(inside, value, -1e30)

    pl.semaphore_wait(barrier, RINGZ - 1 + SHARDS - 1 + SHARDS)

    swaps = [
        copy_to(src, dst.at[y, x], swap_send.at[i], swap_recv.at[i], {"section": other})
        for i, (src, dst) in enumerate(
            ((w_gate.at[0], gate_w), (w_up.at[0], up_w), (w_down.at[0], down_w))
        )
    ]
    swaps.append(copy_to(ffn_gain, gain_in, swap_send.at[3], swap_recv.at[3], {"section": other}))
    for swap in swaps:
        swap.start()

    hand = copy_to(handed, ffn_in, hand_send.at[0], hand_recv.at[0], {"section": other})

    def put_normed(rows_ref, gain, blocks):
        for c in range(2):
            value = normed(rows_ref[c].astype(F32), gain[...])
            blocks[2 * z + c] = value.astype(BF16)

    def attention():
        put_normed(attn_in, attn_gain, attn_rows)
        sent = gather_rows(z, attn_rows, ag_send, ag_recv)
        for load in loads[:3]:
            load.wait()

        @pl.loop(0, 4)
        def _(step):
            span = pl.ds(pl.multiple_of(step * 1024, 1024), 1024)
            rows = attn_rows[:, :, span].reshape(SEQ, 1024)
            for n, weight in enumerate((query_w, key_w, value_w)):
                cols = slice(n * 256, (n + 1) * 256)
                product = jnp.dot(rows, weight[span, :], preferred_element_type=F32)
                sums[:, cols] = jnp.where(step == 0, 0.0, sums[:, cols]) + product

        queries[...] = sums[:, 0:256].astype(BF16)
        keys[...] = sums[:, 256:512].astype(BF16)
        values[...] = sums[:, 512:768].astype(BF16)

        lane = lax.broadcasted_iota(jnp.int32, (SEQ, 128), 1)

        @pl.loop(0, HEADS // 2)
        def _(pair):
            cols = pl.ds(pl.multiple_of(pair * 128, 128), 128)
            query_pair, key_pair, value_pair = queries[:, cols], keys[:, cols], values[:, cols]
            results = []
            for sub in range(2):
                mine = (lane >= 64) if sub else (lane < 64)
                one = jnp.where(mine, query_pair.astype(F32), 0.0).astype(BF16)
                scores = lax.dot_general(
                    one, key_pair, (((1,), (1,)), ((), ())), preferred_element_type=F32
                )
                scores = scores + bias[pair * 2 + sub]
                weights = jnp.exp(scores - jnp.max(scores, axis=-1, keepdims=True))
                probabilities = (weights / jnp.sum(weights, axis=-1, keepdims=True)).astype(BF16)
                results.append(jnp.dot(probabilities, value_pair, preferred_element_type=F32))
            context[:, cols] = jnp.where(lane < 64, results[0], results[1]).astype(BF16)

        loads[3].wait()

        @pl.loop(0, 4)
        def _(step):
            span = pl.ds(pl.multiple_of(step * 1024, 1024), 1024)
            product = jnp.dot(context[...], out_w[:, span], preferred_element_type=F32)
            attn_parts[:, :, span] = product.astype(BF16).reshape(2 * RINGZ, CHUNK, 1024)

        more, total = sum_rows(z, attn_parts, attn_landed, rs_send, rs_recv)
        for c in range(2):
            handed[c] = (attn_in[c].astype(F32) + total(c)).astype(BF16)
        hand.start()
        for moving in sent + more:
            moving.wait_send()
        hand.wait_send()

    def feed():
        hand.wait_recv()
        put_normed(ffn_in, gain_in, ffn_rows)
        sent = gather_rows(z, ffn_rows, ag_send.at[pl.ds(16, 16)], ag_recv.at[pl.ds(16, 16)])

        @pl.loop(0, SIDE)
        def _(step):
            span = pl.ds(pl.multiple_of(step * 1024, 1024), 1024)
            rows = ffn_rows[:, :, span].reshape(SEQ, 1024)
            for n, weight in enumerate((gate_w, up_w)):
                cols = slice(n * HID, (n + 1) * HID)
                product = jnp.dot(
                    rows, weight[step].reshape(SIDE * DK, HID), preferred_element_type=F32
                )
                sums[:, cols] = jnp.where(step == 0, 0.0, sums[:, cols]) + product

        gate = sums[:, 0:HID]
        curve = jnp.tanh(0.7978845608 * (gate + 0.044715 * gate * gate * gate))
        hidden[...] = (0.5 * gate * (1.0 + curve) * sums[:, HID : 2 * HID]).astype(BF16)

        @pl.loop(0, SHARDS)
        def _(step):
            span = pl.ds(pl.multiple_of(step * DK, DK), DK)
            product = jnp.dot(
                hidden[...],
                down_w[step // SIDE, lax.rem(step, SIDE)],
                preferred_element_type=F32,
            )
            ffn_parts[:, :, span] = product.astype(BF16).reshape(2 * RINGZ, CHUNK, DK)

        more, total = sum_rows(
            z, ffn_parts, ffn_landed, rs_send.at[pl.ds(16, 16)], rs_recv.at[pl.ds(16, 16)]
        )
        for c in range(2):
            value = (ffn_in[c].astype(F32) + total(c)).astype(BF16)
            attn_in[c] = value
        for moving in sent + more:
            moving.wait_send()

    @pl.when(section == 0)
    def _():
        attn_in[...] = embeds[0].reshape(2, CHUNK, WIDTH)

    @pl.loop(0, 3)
    def _(turn):
        role = lax.rem(turn + section, 3)

        @pl.when(role == 0)
        def _():
            attention()

        @pl.when(role == 1)
        def _():
            for swap in swaps:
                swap.wait_recv()
            gather_weights(y, x, gate_w, up_w, down_w, w_send, w_recv)

        @pl.when(role == 2)
        def _():
            feed()

    for swap in swaps:
        swap.wait_send()
    loads[4].wait()

    @pl.when(section == 0)
    def _():
        finished = normed(attn_in[...].reshape(ROWS, WIDTH).astype(F32), final_gain[...])
        part = jnp.dot(member_here[...], finished, precision=HIGHEST, preferred_element_type=F32)
        for d in range(RINGZ):
            pooled[d] = part[:, d * PCOLS : (d + 1) * PCOLS]
        pooled_in[z] = pooled[z]

        def pool_copy(k):
            to = lax.rem(z + k, RINGZ)
            return copy_to(
                pooled.at[to], pooled_in.at[z], pool_send.at[k], pool_recv.at[k], {"tensor": to}
            )

        for k in range(1, RINGZ):
            pool_copy(k).start()
        for k in range(1, RINGZ):
            pool_copy(k).wait_recv()
        means = (jnp.sum(pooled_in[...], axis=0) / counts).astype(BF16)
        shares[z] = jnp.dot(means, proj_w[...], preferred_element_type=F32)

        def share_copy(k):
            to = lax.rem(z + k, RINGZ)
            return copy_to(
                shares.at[z], shares.at[z], share_send.at[k], share_recv.at[k], {"tensor": to}
            )

        for k in range(1, RINGZ):
            share_copy(k).start()
        for k in range(1, RINGZ):
            share_copy(k).wait_recv()
        projected = shares[0]
        for d in range(1, RINGZ):
            projected = projected + shares[d]
        mean_square = jnp.mean(projected * projected, axis=-1, keepdims=True)
        unit = (projected * lax.rsqrt(mean_square + EPS)).astype(BF16).astype(F32)
        row = lax.broadcasted_iota(jnp.int32, (2 * SHARDS * 8, PPM), 0)
        chosen = (dest_shard[...] == (row >> 3)) & (dest_slot[...] == (row & 3))
        chosen = chosen.astype(F32)
        lower = jnp.dot(chosen, unit[:, :HALF], preferred_element_type=F32)
        upper = jnp.dot(chosen, unit[:, HALF:], preferred_element_type=F32)
        row = lax.broadcasted_iota(jnp.int32, (2 * SHARDS * 8, HALF), 0)
        blocks = jnp.where((row & 7) < 4, lower, upper)
        placed[...] = blocks.reshape(2 * SHARDS, 8, HALF)
        placed_in[shard] = placed[shard]

        @pl.loop(1, SHARDS)
        def _(k):
            to = lax.rem(shard + k, SHARDS)
            copy_to(
                placed.at[to], placed_in.at[shard], place_send.at[k], place_recv.at[k], {"shard": to}
            ).start()

        @pl.loop(0, SHARDS)
        def _(k):
            to = lax.rem(shard + k, SHARDS)
            copy_to(
                placed.at[SHARDS + to],
                placed_in.at[shard],
                place_send.at[SHARDS + k],
                place_recv.at[k],
                {"section": other, "shard": to},
            ).start()

        for k in range(1, RINGZ):
            pool_copy(k).wait_send()
            share_copy(k).wait_send()

        @pl.loop(1, SHARDS)
        def _(k):
            copy_to(
                placed.at[0], placed_in.at[0], place_send.at[k], place_recv.at[k], {"shard": shard}
            ).wait_recv()

        @pl.loop(1, 2 * SHARDS)
        def _(k):
            copy_to(
                placed.at[0], placed_in.at[0], place_send.at[k], place_recv.at[0], {"shard": shard}
            ).wait_send()

    @pl.when(section == 1)
    def _():
        @pl.loop(0, SHARDS)
        def _(k):
            copy_to(
                placed.at[0], placed_in.at[0], place_send.at[k], place_recv.at[k], {"shard": shard}
            ).wait_recv()

    rows = jnp.sum(placed_in[...], axis=0)
    index[:, 0:HALF] = rows[0:4].astype(BF16)
    index[:, HALF:EMB] = rows[4:8].astype(BF16)


def on_device(
    embeds,
    segments,
    rel_table,
    attn_gain,
    w_query,
    w_key,
    w_value,
    w_out,
    ffn_gain,
    w_gate,
    w_up,
    w_down,
    final_gain,
    w_proj,
    dest_shard,
    dest_slot,
):
    vmem = pl.BlockSpec(memory_space=pltpu.VMEM)
    smem = pl.BlockSpec(memory_space=pltpu.SMEM)
    anywhere = pl.BlockSpec(memory_space=pl.ANY)
    dma = pltpu.SemaphoreType.DMA
    scratch = [
        pltpu.VMEM((WIDTH, 256), BF16),
        pltpu.VMEM((WIDTH, 256), BF16),
        pltpu.VMEM((WIDTH, 256), BF16),
        pltpu.VMEM((256, WIDTH), BF16),
        pltpu.VMEM((PCOLS, EMB), BF16),
        pltpu.VMEM((SIDE, SIDE, DK, HID), BF16),
        pltpu.VMEM((SIDE, SIDE, DK, HID), BF16),
        pltpu.VMEM((SIDE, SIDE, HID, DK), BF16),
        pltpu.VMEM((HEADS, SEQ, SEQ), F32),
        pltpu.VMEM((PPM, ROWS), F32),
        pltpu.VMEM((2 * RINGZ, CHUNK, WIDTH), BF16),
        pltpu.VMEM((2 * RINGZ, CHUNK, WIDTH), BF16),
        pltpu.VMEM((2 * RINGZ, CHUNK, WIDTH), BF16),
        pltpu.VMEM((2 * RINGZ, CHUNK, WIDTH), BF16),
        pltpu.VMEM((2 * RINGZ, CHUNK, WIDTH), BF16),
        pltpu.VMEM((2 * RINGZ, CHUNK, WIDTH), BF16),
        pltpu.VMEM((2, CHUNK, WIDTH), BF16),
        pltpu.VMEM((2, CHUNK, WIDTH), BF16),
        pltpu.VMEM((2, CHUNK, WIDTH), BF16),
        pltpu.VMEM((1, WIDTH), F32),
        pltpu.VMEM((SEQ, 256), BF16),
        pltpu.VMEM((SEQ, 256), BF16),
        pltpu.VMEM((SEQ, 256), BF16),
        pltpu.VMEM((SEQ, 256), BF16),
        pltpu.VMEM((SEQ, 2 * HID), F32),
        pltpu.VMEM((SEQ, HID), BF16),
        pltpu.VMEM((RINGZ, PPM, PCOLS), F32),
        pltpu.VMEM((RINGZ, PPM, PCOLS), F32),
        pltpu.VMEM((RINGZ, PPM, EMB), F32),
        pltpu.VMEM((2 * SHARDS, 8, HALF), F32),
        pltpu.VMEM((SHARDS, 8, HALF), F32),
        dma((5,)),
        dma((4,)),
        dma((4,)),
        dma((1,)),
        dma((1,)),
        dma((32,)),
        dma((32,)),
        dma((32,)),
        dma((32,)),
        dma((32,)),
        dma((32,)),
        dma((RINGZ,)),
        dma((RINGZ,)),
        dma((RINGZ,)),
        dma((RINGZ,)),
        dma((2 * SHARDS,)),
        dma((SHARDS,)),
    ]
    return pl.pallas_call(
        kernel,
        out_shape=jax.ShapeDtypeStruct((4, EMB), BF16),
        in_specs=[
            vmem,
            vmem,
            smem,
            smem,
            vmem,
            anywhere,
            anywhere,
            anywhere,
            anywhere,
            vmem,
            anywhere,
            anywhere,
            anywhere,
            vmem,
            anywhere,
            vmem,
            vmem,
        ],
        out_specs=vmem,
        scratch_shapes=scratch,
        compiler_params=pltpu.CompilerParams(
            collective_id=0, has_side_effects=True, vmem_limit_bytes=58 * 1024 * 1024
        ),
    )(
        embeds,
        segments,
        segments,
        rel_table,
        attn_gain,
        w_query,
        w_key,
        w_value,
        w_out,
        ffn_gain,
        w_gate,
        w_up,
        w_down,
        final_gain.reshape(1, -1),
        w_proj,
        dest_shard,
        dest_slot,
    )


def solution(mesh):
    in_specs = (
        P("shard", "tensor", None),
        P("shard", None),
        P(None, "tensor"),
        P("section", None),
        P("section", None, "tensor"),
        P("section", None, "tensor"),
        P("section", None, "tensor"),
        P("section", "tensor", None),
        P("section", None),
        P("section", "shard", "tensor"),
        P("section", "shard", "tensor"),
        P("section", "tensor", "shard"),
        P(),
        P("tensor", None),
        P("shard", None),
        P("shard", None),
    )
    out_specs = P(("section", "shard"), None)
    return jax.shard_map(
        on_device, mesh=mesh, in_specs=in_specs, out_specs=out_specs, check_vma=False
    )
```

time: 915 us -> 207 us (0.23)
  waiting for transfers between devices: 791 us -> 0 us
  Pallas kernels: 0 us -> 204 us
  matrix products: 60 us -> 0 us
  other arithmetic: 19.9 us -> 0 us
  blocking collectives: 18.1 us -> 0 us
  between operations: 14.3 us -> 0.01 us
    psum x4 -> x0, waiting for transfers between devices: 324 us -> none  [total_rows_sum(): lax.psum(partial_value.astype(jnp.bfloat16), 'tensor').astype(jnp.float32)]
    all_gather x5 -> x0, waiting for transfers between devices: 270 us -> none  [the longest x2 76.8 us: run_layer(): whole_rows = lax.all_gather(rows_in, 'tensor', axis=0, tiled=True)]
    pallas_call x0 -> x1, Pallas kernels: none -> 204 us  [on_device(): pl.pallas_call(kernel, out_shape=jax.ShapeDtypeStruct((4, EMB), BF16), in...]
    unnamed x8 -> x0, waiting for transfers between devices: 156 us -> none
    dot_general x20 -> x0, matrix products: 58.1 us -> none  [the longest x2 19.3 us: feed(): return jnp.dot(activation, full_down, preferred_element_type=jnp.float32)]
    reduce_scatter x1 -> x0, waiting for transfers between devices: 31.5 us -> none  [on_device(): lax.psum_scatter(pooled.reshape(batches * passages, model_width).astype(j...]
    all_gather x1 -> x0, blocking collectives: 18.1 us -> none  [on_device(): projected = lax.all_gather(projected_cols, 'tensor', axis=1, tiled=True)]
    convert_element_type x3 -> x0, other arithmetic: 9.34 us -> none  [the longest x2 8.7 us: run_layer(): finished_rows = (middle.astype(jnp.float32) + fed).astype(jnp.bfloat16)]
  transfers between devices with their start and end apart: 14 -> 0, of which waited for: 14 -> 0; matrix products, arithmetic and copies ran while one was open for 1% -> 0% of each run, Pallas kernels for 0% -> 0%
where the time goes in v1:
time: 207 us
  Pallas kernels  204 us (99%)
  local copies, waits for them, and re-layouts  2.64 us (1%)
    pallas_call x1, Pallas kernels, on_device(): pl.pallas_call(kernel, out_shape=jax.ShapeDtypeStruct((4, EMB), BF16), in...  204 us

profile of v1, /device:TPU:1, one launch (start us, length us, event | category | flops | bytes accessed | tf_op | source)
XLA Modules:
  0.0 206.9 jit_solution(9050051191731868515)
XLA Ops:
  0.0 1.4 copy.17.rel_s
  1.4 204.3 %shard_map.154 = bf16[4,768]{1,0:T(4,128)(2,1)} custom-call(bf16[1,32,4096]{2,1,0:T(8,128)(2,1)} %embeds.1, s32[1,256]{1,0:T(1,128)} %segments_s.1, s32[1,256]{1,0:T(1,128)} %segments_s.1, f32[32,4]{1,0:T(8,128)} %copy.17.rel_s, f32[1,4096]{1,0:T(1,128)} %attn_gain.1, bf16[1,4096,256]{2,1,0:T(8,128)(2,1)} %w_query.1, bf16[1,4096,256]{2,1,0:T(8,128)(2,1)} %w_key.1, ...), custom_call_target="tpu_custom_call" | custom-call | tf_op jit(solution)/shard_map/pallas_call | solution.py:657
  205.6 1.3 copy.19

commit v2 on v1

v2 whole, which is shorter than its diff:
```python
import jax
import jax.numpy as jnp
from jax import lax
from jax.experimental import pallas as pl
from jax.experimental.pallas import tpu as pltpu
from jax.sharding import PartitionSpec as P

MESH = pl.DeviceIdType.MESH
F32 = jnp.float32
BF16 = jnp.bfloat16
HIGHEST = lax.Precision.HIGHEST

ROWS = 32
CHUNK = 16
RINGZ = 8
SIDE = 4
SHARDS = SIDE * SIDE
WIDTH = 4096
GROUPS = 8
COLS = WIDTH // GROUPS
SEQ = 256
MID = SEQ // 2
HEADS = 4
PPM = 8
DK = 256
HID = 640
EMB = 768
HALF = EMB // 2
EPS = 1e-06

ORDER = (0, 1, 7, 2, 6, 3, 5, 4)
PLACE = tuple(ORDER.index(slot) for slot in range(RINGZ))
lowest = (0, 1, 2, 3, 4, 5, 6, 7, 8, 12, 16, 23, 32, 46, 64, 91)


def copy_to(src, dst, send, recv, device):
    return pltpu.make_async_remote_copy(
        src_ref=src,
        dst_ref=dst,
        send_sem=send,
        recv_sem=recv,
        device_id=device,
        device_id_type=MESH,
    )


def part_rows(half):
    return pl.ds(half * CHUNK, CHUNK)


def group_cols(g):
    return pl.ds(pl.multiple_of(g * COLS, COLS), COLS)


class Spread:
    def __init__(self, z, rows, send, recv):
        self.beside = (lax.rem(z + 1, RINGZ), lax.rem(z + RINGZ - 1, RINGZ))
        self.rows, self.send, self.recv = rows, send, recv

    def move(self, way, hop, g, src=None, section=None):
        source, target = (RINGZ - hop + 1, RINGZ - hop) if way == 0 else (hop - 1, hop)
        rows = pl.ds(0, ROWS) if hop < 4 else part_rows(way)
        if src is None:
            src = self.rows.at[g, PLACE[source % RINGZ], rows]
        device = {"tensor": self.beside[way]}
        if section is not None:
            device["section"] = section
        at = way * 4 + hop - 1
        return copy_to(
            src,
            self.rows.at[g, PLACE[target % RINGZ], rows],
            self.send.at[at, g],
            self.recv.at[at, g],
            device,
        )

    def step(self, hop, g):
        for way in (0, 1):
            if hop > 1:
                self.move(way, hop - 1, g).wait_recv()
            self.move(way, hop, g).start()

    def land(self, g):
        for way in (0, 1):
            self.move(way, 4, g).wait_recv()

    def sent(self, g, hops):
        for way in (0, 1):
            for hop in hops:
                self.move(way, hop, g).wait_send()


class Chains:
    def __init__(self, z, parts, landed, send, recv):
        self.beside = (lax.rem(z + 1, RINGZ), lax.rem(z + RINGZ - 1, RINGZ))
        self.parts, self.landed, self.send, self.recv = parts, landed, send, recv

    def move(self, way, hop, g, half):
        ahead = 5 - hop
        place = PLACE[ahead if way == 0 else RINGZ - ahead]
        at = way * 8 + (hop - 1) * 2 + half
        rows = part_rows(half)
        return copy_to(
            self.parts.at[g, place, rows],
            self.landed.at[way, hop - 1, g, rows],
            self.send.at[at, g],
            self.recv.at[at, g],
            {"tensor": self.beside[way]},
        )

    def forward(self, hop, g, late):
        for way in (0, 1):
            half = way if late else 1 - way
            if hop > (1 if late else 2):
                self.move(way, hop - 1, g, half).wait_recv()
                place = PLACE[5 - hop if way == 0 else RINGZ - 5 + hop]
                rows = part_rows(half)
                total = self.parts[g, place, rows].astype(F32) + self.landed[
                    way, hop - 2, g, rows
                ].astype(F32)
                self.parts[g, place, rows] = total.astype(BF16)
            self.move(way, hop, g, half).start()

    def total(self, g):
        for way in (0, 1):
            for half in (0, 1):
                self.move(way, 4, g, half).wait_recv()
        own = self.parts[g, 0].astype(F32)
        return own + self.landed[0, 3, g].astype(F32) + self.landed[1, 3, g].astype(F32)

    def sent(self, g):
        for way in (0, 1):
            self.move(way, 1, g, way).wait_send()
            for hop in (2, 3, 4):
                for half in (0, 1):
                    self.move(way, hop, g, half).wait_send()


class Weights:
    def __init__(self, y, x, gate, up, down, send, recv):
        self.y, self.x = y, x
        self.arrays = ((gate, 0, DK), (up, 0, DK), (down, 0, HID // 2), (down, HID // 2, HID // 2))
        self.send, self.recv = send, recv

    def piece(self, array, first, second, sign):
        ref, start, size = self.arrays[array]
        if sign is not None:
            size = size // 2
            start = start + sign * size
        along_x, along_y = (first, second) if array % 2 == 0 else (second, first)
        at_x, at_y = lax.rem(self.x + along_x, SIDE), lax.rem(self.y + along_y, SIDE)
        return ref.at[at_y, at_x, pl.ds(start, size)]

    def copy(self, array, stage, hop, line, sign, landing):
        step = 1 if sign == 0 else SIDE - 1
        back = SIDE - step
        away = (back if hop == 1 else 0) + (back if landing else 0)
        if stage == 0:
            ref = self.piece(array, away % SIDE, 0, None if hop == 0 else sign)
            at = hop * 2 + sign
        else:
            ref = self.piece(array, line, away % SIDE, None if hop == 0 else sign)
            at = 4 + (line * 2 + hop) * 2 + sign
        on_x = (array % 2 == 0) == (stage == 0)
        if on_x:
            shard = self.y * SIDE + lax.rem(self.x + step, SIDE)
        else:
            shard = lax.rem(self.y + step, SIDE) * SIDE + self.x
        return copy_to(ref, ref, self.send.at[array, at], self.recv.at[array, at], {"shard": shard})

    def go(self, array, stage, hop, line, sign):
        self.copy(array, stage, hop, line, sign, False).start()

    def wait(self, array, stage, hop, line, sign):
        self.copy(array, stage, hop, line, sign, True).wait_recv()

    def run(self, ready):
        both = (0, 1)
        for array in range(4):
            ready(array)
            for sign in both:
                self.go(array, 0, 0, 0, sign)
                self.go(array, 1, 0, 0, sign)
        for array in range(4):
            for sign in both:
                self.wait(array, 0, 0, 0, sign)
                self.go(array, 0, 1, 0, sign)
                line = SIDE - 1 if sign == 0 else 1
                for other in both:
                    self.go(array, 1, 0, line, other)
        for array in range(4):
            for sign in both:
                self.wait(array, 0, 1, 0, sign)
            for sign in both:
                self.go(array, 1, 0, 2, sign)
        for array in range(4):
            for line in (0, 1, 3, 2):
                for sign in both:
                    self.wait(array, 1, 0, line, sign)
                    self.go(array, 1, 1, line, sign)

    def land(self, arrays):
        for array in arrays:
            for line in range(SIDE):
                for sign in (0, 1):
                    self.wait(array, 1, 1, line, sign)

    def sent(self):
        for array in range(4):
            for sign in (0, 1):
                for hop in (0, 1):
                    self.copy(array, 0, hop, 0, sign, False).wait_send()
                    for line in range(SIDE):
                        self.copy(array, 1, hop, line, sign, False).wait_send()


def kernel(
    embeds,
    segments,
    rel_table,
    attn_gain,
    w_query,
    w_key,
    w_value,
    w_out,
    ffn_gain,
    w_gate,
    w_up,
    w_down,
    final_gain,
    w_proj,
    dest_shard,
    dest_slot,
    index,
    query_w,
    key_w,
    value_w,
    out_w,
    proj_w,
    gate_w,
    up_w,
    down_w,
    bias,
    member_here,
    attn_rows,
    attn_parts,
    attn_landed,
    ffn_rows,
    ffn_parts,
    ffn_landed,
    attn_in,
    handed,
    ffn_in,
    staged,
    queries,
    keys,
    values,
    context,
    sums,
    hidden,
    pooled,
    pooled_in,
    shares,
    placed,
    placed_in,
    load_sem,
    swap_send,
    swap_recv,
    hand_send,
    hand_recv,
    near_send,
    near_recv,
    ag_send,
    ag_recv,
    rs_send,
    rs_recv,
    w_send,
    w_recv,
    pool_send,
    pool_recv,
    share_send,
    share_recv,
    place_send,
    place_recv,
    free_sem,
):
    section = lax.axis_index("section")
    z = lax.axis_index("tensor")
    shard = lax.axis_index("shard")
    y, x = shard // SIDE, lax.rem(shard, SIDE)
    other = 1 - section

    barrier = pltpu.get_barrier_semaphore()

    def greet(device):
        pl.semaphore_signal(barrier, inc=1, device_id=device, device_id_type=MESH)

    @pl.loop(1, SHARDS)
    def _(k):
        greet({"shard": lax.rem(shard + k, SHARDS)})

    @pl.loop(0, SHARDS)
    def _(k):
        greet({"section": other, "shard": lax.rem(shard + k, SHARDS)})

    @pl.loop(1, RINGZ)
    def _(k):
        greet({"tensor": lax.rem(z + k, RINGZ)})

    for k in (1, RINGZ - 1):
        greet({"section": other, "tensor": lax.rem(z + k, RINGZ)})

    loads = [
        pltpu.make_async_copy(src, dst, load_sem.at[i])
        for i, (src, dst) in enumerate(
            (
                (w_query.at[0], query_w),
                (w_key.at[0], key_w),
                (w_value.at[0], value_w),
                (w_out.at[0], out_w),
                (w_proj, proj_w),
            )
        )
    ]
    for load in loads:
        load.start()

    passage = lax.broadcasted_iota(jnp.int32, (PPM, SEQ), 0)
    counts = jnp.sum((segments[...] == passage).astype(F32), axis=-1, keepdims=True)
    first = jnp.sum((segments[...] < passage).astype(F32), axis=-1, keepdims=True)

    def members(token):
        at = token.astype(F32)
        return ((at >= first) & (at < first + counts)).astype(F32)

    lane = lax.broadcasted_iota(jnp.int32, (PPM, ROWS), 1)
    member_here[...] = members(lane + z * ROWS)

    def slots(place):
        slot = jnp.full_like(place, ORDER[0])
        for at in range(1, RINGZ):
            slot = jnp.where(place == at, ORDER[at], slot)
        return slot

    def tokens(position):
        return (((slots(position >> 5) + z) & 7) << 5) + (position & 31)

    lane = lax.broadcasted_iota(jnp.int32, (PPM, SEQ), 1)
    member = members(tokens(lane)).astype(BF16)
    bias[0] = lax.dot_general(
        member, member, (((0,), (0,)), ((), ())), preferred_element_type=F32
    )

    @pl.loop(0, RINGZ)
    def _(block):
        rows = pl.ds(pl.multiple_of(block * ROWS, ROWS), ROWS)
        inside = bias[0, rows, :] > 0.5
        i = tokens(lax.broadcasted_iota(jnp.int32, (ROWS, SEQ), 0) + block * ROWS)
        k = tokens(lax.broadcasted_iota(jnp.int32, (ROWS, SEQ), 1))
        ahead = k - i
        distance = jnp.abs(ahead)
        for head in range(HEADS):
            before = jnp.broadcast_to(rel_table[0:1, head : head + 1], (ROWS, SEQ))
            after = jnp.broadcast_to(rel_table[16:17, head : head + 1], (ROWS, SEQ))
            for code in range(1, 16):
                reached = distance >= lowest[code]
                before = jnp.where(reached, rel_table[code : code + 1, head : head + 1], before)
                after = jnp.where(
                    reached, rel_table[16 + code : 17 + code, head : head + 1], after
                )
            value = jnp.where(ahead > 0, after, before)
            bias[head, rows, :] = jnp.where(inside, value, -1e30)

    @pl.when(section == 0)
    def _():
        for g in range(GROUPS):
            attn_in[g] = embeds[0, :, g * COLS : (g + 1) * COLS]

    pl.semaphore_wait(barrier, RINGZ - 1 + SHARDS - 1 + SHARDS + 2)

    swaps = [
        copy_to(src, dst, swap_send.at[i], swap_recv.at[i], {"section": other})
        for i, (src, dst) in enumerate(
            (
                (w_gate.at[0], gate_w.at[y, x]),
                (w_up.at[0], up_w.at[y, x]),
                (w_down.at[0], down_w.at[y, x]),
            )
        )
    ]
    for swap in swaps:
        swap.start()

    attn_spread = Spread(z, attn_rows, ag_send.at[0], ag_recv.at[0])
    ffn_spread = Spread(z, ffn_rows, ag_send.at[1], ag_recv.at[1])
    attn_chains = Chains(z, attn_parts, attn_landed, rs_send.at[0], rs_recv.at[0])
    ffn_chains = Chains(z, ffn_parts, ffn_landed, rs_send.at[1], rs_recv.at[1])
    weights = Weights(y, x, gate_w, up_w, down_w, w_send, w_recv)
    hand = copy_to(handed, ffn_in, hand_send.at[0], hand_recv.at[0], {"section": other})

    def near(g):
        return copy_to(
            staged.at[g], ffn_rows.at[g, 0], near_send.at[g], near_recv.at[g], {"section": other}
        )

    def squares(value):
        return jnp.sum(value * value, axis=-1, keepdims=True)

    def scale_of(total):
        return lax.rsqrt(total * (1.0 / WIDTH) + EPS)

    no_squares = jnp.zeros((ROWS, 1), F32)

    def run_spread(spread, multiply):
        @pl.loop(0, GROUPS)
        def _(g):
            spread.step(2, g)

        @pl.loop(0, GROUPS)
        def _(g):
            spread.step(3, g)

        @pl.loop(0, GROUPS // 2)
        def _(pair):
            multiply(pair, 0)
            for g in (2 * pair, 2 * pair + 1):
                spread.step(4, g)

    def run_chains(chains, far, between, close):
        @pl.loop(0, GROUPS)
        def _(g):
            far(g)
            chains.forward(1, g, True)
            chains.forward(2, g, False)

        between()

        @pl.loop(0, GROUPS)
        def _(g):
            close(g)
            chains.forward(2, g, True)
            chains.forward(3, g, False)

        @pl.loop(0, GROUPS)
        def _(g):
            chains.forward(3, g, True)
            chains.forward(4, g, False)

        @pl.loop(0, GROUPS)
        def _(g):
            chains.forward(4, g, True)

    def finish(chains, before, after):
        def add(g, total):
            value = (before[g].astype(F32) + chains.total(g)).astype(BF16)
            after[g] = value
            return total + squares(value.astype(F32))

        return lax.fori_loop(0, GROUPS, add, no_squares)

    def half(place):
        return pl.ds(place * 4, 4), slice(place * MID, (place + 1) * MID)

    def attention():
        total = lax.fori_loop(
            0, GROUPS, lambda g, t: t + squares(attn_in[g].astype(F32)), no_squares
        )
        scale = scale_of(total)

        @pl.loop(0, GROUPS)
        def _(g):
            value = attn_in[g].astype(F32) * scale * attn_gain[:, group_cols(g)]
            attn_rows[g, 0] = value.astype(BF16)
            attn_spread.step(1, g)

        for load in loads[:3]:
            load.wait()

        def multiply(pair, place):
            blocks, rows = half(place)
            for n, weight in enumerate((query_w, key_w, value_w)):
                cols = slice(n * 256, (n + 1) * 256)
                product = jnp.where(pair == 0, 0.0, sums[rows, cols])
                for g in (2 * pair, 2 * pair + 1):
                    product = product + jnp.dot(
                        attn_rows[g, blocks].reshape(MID, COLS),
                        weight[group_cols(g), :],
                        preferred_element_type=F32,
                    )
                sums[rows, cols] = product

        run_spread(attn_spread, multiply)

        @pl.loop(0, GROUPS)
        def _(g):
            attn_spread.land(g)

        @pl.loop(0, GROUPS // 2)
        def _(pair):
            multiply(pair, 1)

        queries[...] = sums[:, 0:256].astype(BF16)
        keys[...] = sums[:, 256:512].astype(BF16)
        values[...] = sums[:, 512:768].astype(BF16)

        def attend(place):
            _, rows = half(place)
            head_lane = lax.broadcasted_iota(jnp.int32, (MID, 128), 1)

            @pl.loop(0, HEADS // 2)
            def _(pair):
                cols = pl.ds(pl.multiple_of(pair * 128, 128), 128)
                query_pair, key_pair, value_pair = queries[rows, cols], keys[:, cols], values[:, cols]
                results = []
                for sub in range(2):
                    mine = (head_lane >= 64) if sub else (head_lane < 64)
                    one = jnp.where(mine, query_pair.astype(F32), 0.0).astype(BF16)
                    scores = lax.dot_general(
                        one, key_pair, (((1,), (1,)), ((), ())), preferred_element_type=F32
                    )
                    scores = scores + bias[pair * 2 + sub, rows, :]
                    powers = jnp.exp(scores - jnp.max(scores, axis=-1, keepdims=True))
                    shares_of = powers / jnp.sum(powers, axis=-1, keepdims=True)
                    results.append(
                        jnp.dot(shares_of.astype(BF16), value_pair, preferred_element_type=F32)
                    )
                context[rows, cols] = jnp.where(head_lane < 64, results[0], results[1]).astype(BF16)

        def project(g, place):
            blocks, rows = half(place)
            product = jnp.dot(
                context[rows, :], out_w[:, group_cols(g)], preferred_element_type=F32
            )
            attn_parts[g, blocks] = product.astype(BF16).reshape(4, ROWS, COLS)

        attend(1)
        loads[3].wait()
        run_chains(
            attn_chains, lambda g: project(g, 1), lambda: attend(0), lambda g: project(g, 0)
        )
        scale = scale_of(finish(attn_chains, attn_in, handed))

        @pl.loop(0, GROUPS)
        def _(g):
            value = handed[g].astype(F32) * scale * ffn_gain[:, group_cols(g)]
            staged[g] = value.astype(BF16)
            for way in (0, 1):
                ffn_spread.move(way, 1, g, staged.at[g], other).start()
            near(g).start()

        hand.start()

    def feed():
        def multiply(pair, place):
            blocks, rows = half(place)
            for n, weight in enumerate((gate_w, up_w)):
                cols = slice(n * HID, (n + 1) * HID)
                product = jnp.where(pair == 0, 0.0, sums[rows, cols])
                for j in range(2):
                    product = product + jnp.dot(
                        ffn_rows[2 * pair + j, blocks].reshape(MID, COLS),
                        weight[pair, 2 * j : 2 * j + 2].reshape(COLS, HID),
                        preferred_element_type=F32,
                    )
                sums[rows, cols] = product

        def activate(place):
            _, rows = half(place)
            gate = sums[rows, 0:HID]
            curve = jnp.tanh(0.7978845608 * (gate + 0.044715 * gate * gate * gate))
            hidden[rows, :] = (0.5 * gate * (1.0 + curve) * sums[rows, HID : 2 * HID]).astype(BF16)

        def first_multiply(pair, place):
            @pl.when(pair == 0)
            def _():
                @pl.loop(0, GROUPS)
                def _(g):
                    near(g).wait_recv()

                weights.land((0, 1))

            multiply(pair, place)

        run_spread(ffn_spread, first_multiply)
        activate(0)

        @pl.loop(0, GROUPS)
        def _(g):
            ffn_spread.land(g)

        @pl.loop(0, GROUPS // 2)
        def _(pair):
            multiply(pair, 1)

        activate(1)
        weights.land((2, 3))

        def project(g, place):
            blocks, rows = half(place)
            for j in range(2):
                product = jnp.dot(
                    hidden[rows, :],
                    down_w[g // 2, 2 * lax.rem(g, 2) + j],
                    preferred_element_type=F32,
                )
                ffn_parts[g, blocks, :, j * DK : (j + 1) * DK] = product.astype(BF16).reshape(
                    4, ROWS, DK
                )

        run_chains(ffn_chains, lambda g: project(g, 1), lambda: None, lambda g: project(g, 0))
        hand.wait_recv()
        finish(ffn_chains, ffn_in, attn_in)

    @pl.loop(0, 3)
    def _(turn):
        role = lax.rem(turn + section, 3)

        @pl.when(role == 0)
        def _():
            attention()

        @pl.when(role == 1)
        def _():
            @pl.when(section == 0)
            def _():
                pl.semaphore_wait(free_sem, 1)

            def ready(array):
                if array < 3:
                    swaps[array].wait_recv()

            weights.run(ready)

            @pl.when(section == 1)
            def _():
                pl.semaphore_signal(
                    free_sem, inc=1, device_id={"section": other}, device_id_type=MESH
                )

        @pl.when(role == 2)
        def _():
            feed()

    loads[4].wait()

    @pl.when(section == 0)
    def _():
        total = lax.fori_loop(
            0, GROUPS, lambda g, t: t + squares(attn_in[g].astype(F32)), no_squares
        )
        scale = scale_of(total)

        def pool_copy(k):
            to = lax.rem(z + k, RINGZ)
            return copy_to(
                pooled.at[to], pooled_in.at[z], pool_send.at[k], pool_recv.at[k], {"tensor": to}
            )

        def share_copy(k):
            to = lax.rem(z + k, RINGZ)
            return copy_to(
                shares.at[z], shares.at[z], share_send.at[k], share_recv.at[k], {"tensor": to}
            )

        def pool(g):
            finished = attn_in[g].astype(F32) * scale * final_gain[:, group_cols(g)]
            return jnp.dot(
                member_here[...], finished, precision=HIGHEST, preferred_element_type=F32
            )

        for k in (4, 3, 5, 2, 6, 1, 7):
            to = lax.rem(z + k, RINGZ)
            pooled[to] = pool(to)
            pool_copy(k).start()
        pooled_in[z] = pool(z)
        for k in range(1, RINGZ):
            pool_copy(k).wait_recv()
        means = (jnp.sum(pooled_in[...], axis=0) / counts).astype(BF16)
        shares[z] = jnp.dot(means, proj_w[...], preferred_element_type=F32)
        for k in (4, 3, 5, 2, 6, 1, 7):
            share_copy(k).start()
        row = lax.broadcasted_iota(jnp.int32, (2 * SHARDS * 8, PPM), 0)
        chosen = (dest_shard[...] == (row >> 3)) & (dest_slot[...] == (row & 3))
        chosen = chosen.astype(F32)
        for k in range(1, RINGZ):
            share_copy(k).wait_recv()
        projected = shares[0]
        for d in range(1, RINGZ):
            projected = projected + shares[d]
        mean_square = jnp.mean(projected * projected, axis=-1, keepdims=True)
        unit = (projected * lax.rsqrt(mean_square + EPS)).astype(BF16).astype(F32)
        lower = jnp.dot(chosen, unit[:, :HALF], preferred_element_type=F32)
        upper = jnp.dot(chosen, unit[:, HALF:], preferred_element_type=F32)
        row = lax.broadcasted_iota(jnp.int32, (2 * SHARDS * 8, HALF), 0)
        blocks = jnp.where((row & 7) < 4, lower, upper)
        placed[...] = blocks.reshape(2 * SHARDS, 8, HALF)
        placed_in[shard] = placed[shard]

        @pl.loop(1, SHARDS)
        def _(k):
            to = lax.rem(shard + k, SHARDS)
            copy_to(
                placed.at[to], placed_in.at[shard], place_send.at[k], place_recv.at[k], {"shard": to}
            ).start()

        @pl.loop(0, SHARDS)
        def _(k):
            to = lax.rem(shard + k, SHARDS)
            copy_to(
                placed.at[SHARDS + to],
                placed_in.at[shard],
                place_send.at[SHARDS + k],
                place_recv.at[k],
                {"section": other, "shard": to},
            ).start()

    for swap in swaps:
        swap.wait_send()
    weights.sent()
    hand.wait_send()

    @pl.loop(0, GROUPS)
    def _(g):
        attn_spread.sent(g, (1, 2, 3, 4))
        for way in (0, 1):
            ffn_spread.move(way, 1, g, staged.at[g], other).wait_send()
        ffn_spread.sent(g, (2, 3, 4))
        near(g).wait_send()
        attn_chains.sent(g)
        ffn_chains.sent(g)

    def place_wait(k):
        return copy_to(
            placed.at[0], placed_in.at[0], place_send.at[k], place_recv.at[k], {"shard": shard}
        )

    @pl.when(section == 0)
    def _():
        for k in range(1, RINGZ):
            pool_wait = copy_to(
                pooled.at[0], pooled_in.at[0], pool_send.at[k], pool_recv.at[k], {"tensor": z}
            )
            pool_wait.wait_send()
            share_wait = copy_to(
                shares.at[0], shares.at[0], share_send.at[k], share_recv.at[k], {"tensor": z}
            )
            share_wait.wait_send()

        @pl.loop(1, SHARDS)
        def _(k):
            place_wait(k).wait_recv()
            place_wait(k).wait_send()

        @pl.loop(SHARDS, 2 * SHARDS)
        def _(k):
            copy_to(
                placed.at[0], placed_in.at[0], place_send.at[k], place_recv.at[0], {"shard": shard}
            ).wait_send()

    @pl.when(section == 1)
    def _():
        @pl.loop(0, SHARDS)
        def _(k):
            place_wait(k).wait_recv()

    rows = jnp.sum(placed_in[...], axis=0)
    index[:, 0:HALF] = rows[0:4].astype(BF16)
    index[:, HALF:EMB] = rows[4:8].astype(BF16)


def on_device(
    embeds,
    segments,
    rel_table,
    attn_gain,
    w_query,
    w_key,
    w_value,
    w_out,
    ffn_gain,
    w_gate,
    w_up,
    w_down,
    final_gain,
    w_proj,
    dest_shard,
    dest_slot,
):
    vmem = pl.BlockSpec(memory_space=pltpu.VMEM)
    anywhere = pl.BlockSpec(memory_space=pl.ANY)
    dma = pltpu.SemaphoreType.DMA
    rows = pltpu.VMEM((GROUPS, RINGZ, ROWS, COLS), BF16)
    landed = pltpu.VMEM((2, 4, GROUPS, ROWS, COLS), BF16)
    own = pltpu.VMEM((GROUPS, ROWS, COLS), BF16)
    heads = pltpu.VMEM((SEQ, 256), BF16)
    scratch = [
        pltpu.VMEM((WIDTH, 256), BF16),
        pltpu.VMEM((WIDTH, 256), BF16),
        pltpu.VMEM((WIDTH, 256), BF16),
        pltpu.VMEM((256, WIDTH), BF16),
        pltpu.VMEM((COLS, EMB), BF16),
        pltpu.VMEM((SIDE, SIDE, DK, HID), BF16),
        pltpu.VMEM((SIDE, SIDE, DK, HID), BF16),
        pltpu.VMEM((SIDE, SIDE, HID, DK), BF16),
        pltpu.VMEM((HEADS, SEQ, SEQ), F32),
        pltpu.VMEM((PPM, ROWS), F32),
        rows,
        rows,
        landed,
        rows,
        rows,
        landed,
        own,
        own,
        own,
        own,
        heads,
        heads,
        heads,
        heads,
        pltpu.VMEM((SEQ, 2 * HID), F32),
        pltpu.VMEM((SEQ, HID), BF16),
        pltpu.VMEM((RINGZ, PPM, COLS), F32),
        pltpu.VMEM((RINGZ, PPM, COLS), F32),
        pltpu.VMEM((RINGZ, PPM, EMB), F32),
        pltpu.VMEM((2 * SHARDS, 8, HALF), F32),
        pltpu.VMEM((SHARDS, 8, HALF), F32),
        dma((5,)),
        dma((3,)),
        dma((3,)),
        dma((1,)),
        dma((1,)),
        dma((GROUPS,)),
        dma((GROUPS,)),
        dma((2, 8, GROUPS)),
        dma((2, 8, GROUPS)),
        dma((2, 16, GROUPS)),
        dma((2, 16, GROUPS)),
        dma((4, 20)),
        dma((4, 20)),
        dma((RINGZ,)),
        dma((RINGZ,)),
        dma((RINGZ,)),
        dma((RINGZ,)),
        dma((2 * SHARDS,)),
        dma((SHARDS,)),
        pltpu.SemaphoreType.REGULAR,
    ]
    vmem_args = (0, 1, 2, 3, 8, 12, 14, 15)
    return pl.pallas_call(
        kernel,
        out_shape=jax.ShapeDtypeStruct((4, EMB), BF16),
        in_specs=[vmem if i in vmem_args else anywhere for i in range(16)],
        out_specs=vmem,
        scratch_shapes=scratch,
        compiler_params=pltpu.CompilerParams(
            collective_id=0, has_side_effects=True, vmem_limit_bytes=58 * 1024 * 1024
        ),
    )(
        embeds,
        segments,
        rel_table,
        attn_gain,
        w_query,
        w_key,
        w_value,
        w_out,
        ffn_gain,
        w_gate,
        w_up,
        w_down,
        final_gain.reshape(1, -1),
        w_proj,
        dest_shard,
        dest_slot,
    )


def solution(mesh):
    in_specs = (
        P("shard", "tensor", None),
        P("shard", None),
        P(None, "tensor"),
        P("section", None),
        P("section", None, "tensor"),
        P("section", None, "tensor"),
        P("section", None, "tensor"),
        P("section", "tensor", None),
        P("section", None),
        P("section", "shard", "tensor"),
        P("section", "shard", "tensor"),
        P("section", "tensor", "shard"),
        P(),
        P("tensor", None),
        P("shard", None),
        P("shard", None),
    )
    out_specs = P(("section", "shard"), None)
    return jax.shard_map(
        on_device, mesh=mesh, in_specs=in_specs, out_specs=out_specs, check_vma=False
    )
```

time: 207 us -> 176 us (0.85)
  Pallas kernels: 204 us -> 173 us
    pallas_call x1, Pallas kernels: 204 us -> 173 us  [on_device(): pl.pallas_call(kernel, out_shape=jax.ShapeDtypeStruct((4, EMB), BF16), in...]
where the time goes in v2:
time: 176 us
  Pallas kernels  173 us (98%)
  local copies, waits for them, and re-layouts  2.64 us (2%)
    pallas_call x1, Pallas kernels, on_device(): pl.pallas_call(kernel, out_shape=jax.ShapeDtypeStruct((4, EMB), BF16), in...  173 us

profile of v2, /device:TPU:1, one launch (start us, length us, event | category | flops | bytes accessed | tf_op | source)
XLA Modules:
  0.0 175.7 jit_solution(380884541196414055)
XLA Ops:
  0.0 1.4 copy.17.rel_table
  1.4 173.0 %shard_map.154 = bf16[4,768]{1,0:T(4,128)(2,1)} custom-call(bf16[1,32,4096]{2,1,0:T(8,128)(2,1)} %embeds.1, s32[1,256]{1,0:T(1,128)} %segments.1, f32[32,4]{1,0:T(8,128)} %copy.17.rel_table, f32[1,4096]{1,0:T(1,128)} %attn_gain.1, bf16[1,4096,256]{2,1,0:T(8,128)(2,1)} %w_query.1, bf16[1,4096,256]{2,1,0:T(8,128)(2,1)} %w_key.1, ...), custom_call_target="tpu_custom_call" | custom-call | tf_op jit(solution)/shard_map/pallas_call | solution.py:850
  174.4 1.3 copy.19

commit v3 on v2

--- a/solution.py
+++ b/solution.py
@@ -19,7 +19,7 @@
 GROUPS = 8
 COLS = WIDTH // GROUPS
 SEQ = 256
-MID = SEQ // 2
+NEAR = 5
 HEADS = 4
 PPM = 8
 DK = 256
@@ -69,8 +69,8 @@
         return copy_to(
             src,
             self.rows.at[g, PLACE[target % RINGZ], rows],
-            self.send.at[at, g],
-            self.recv.at[at, g],
+            self.send.at[at],
+            self.recv.at[at, 0 if isinstance(g, pl.Slice) else g],
             device,
         )
 
@@ -84,10 +84,11 @@
         for way in (0, 1):
             self.move(way, 4, g).wait_recv()
 
-    def sent(self, g, hops):
+    def sent(self, src=None):
         for way in (0, 1):
-            for hop in hops:
-                self.move(way, hop, g).wait_send()
+            for hop in (1, 2, 3, 4):
+                whole = pl.ds(0, GROUPS)
+                self.move(way, hop, whole, src if hop == 1 else None).wait_send()
 
 
 class Chains:
@@ -103,8 +104,8 @@
         return copy_to(
             self.parts.at[g, place, rows],
             self.landed.at[way, hop - 1, g, rows],
-            self.send.at[at, g],
-            self.recv.at[at, g],
+            self.send.at[at],
+            self.recv.at[at, 0 if isinstance(g, pl.Slice) else g],
             {"tensor": self.beside[way]},
         )
 
@@ -128,12 +129,13 @@
         own = self.parts[g, 0].astype(F32)
         return own + self.landed[0, 3, g].astype(F32) + self.landed[1, 3, g].astype(F32)
 
-    def sent(self, g):
+    def sent(self):
+        whole = pl.ds(0, GROUPS)
         for way in (0, 1):
-            self.move(way, 1, g, way).wait_send()
+            self.move(way, 1, whole, way).wait_send()
             for hop in (2, 3, 4):
                 for half in (0, 1):
-                    self.move(way, hop, g, half).wait_send()
+                    self.move(way, hop, whole, half).wait_send()
 
 
 class Weights:
@@ -232,6 +234,13 @@
     dest_shard,
     dest_slot,
     index,
+    segments_v,
+    rel_v,
+    attn_gain_v,
+    ffn_gain_v,
+    final_gain_v,
+    dest_shard_v,
+    dest_slot_v,
     query_w,
     key_w,
     value_w,
@@ -264,6 +273,7 @@
     placed,
     placed_in,
     load_sem,
+    rows_sem,
     swap_send,
     swap_recv,
     hand_send,
@@ -295,39 +305,57 @@
     def greet(device):
         pl.semaphore_signal(barrier, inc=1, device_id=device, device_id_type=MESH)
 
+    @pl.loop(1, RINGZ)
+    def _(k):
+        greet({"tensor": lax.rem(z + k, RINGZ)})
+
+    @pl.loop(0, RINGZ)
+    def _(k):
+        greet({"section": other, "tensor": lax.rem(z + k, RINGZ)})
+
     @pl.loop(1, SHARDS)
     def _(k):
         greet({"shard": lax.rem(shard + k, SHARDS)})
 
-    @pl.loop(0, SHARDS)
-    def _(k):
-        greet({"section": other, "shard": lax.rem(shard + k, SHARDS)})
-
-    @pl.loop(1, RINGZ)
-    def _(k):
-        greet({"tensor": lax.rem(z + k, RINGZ)})
-
-    for k in (1, RINGZ - 1):
-        greet({"section": other, "tensor": lax.rem(z + k, RINGZ)})
-
+    sources = (
+        (segments, segments_v),
+        (rel_table, rel_v),
+        (attn_gain, attn_gain_v),
+        (w_query.at[0], query_w),
+        (w_key.at[0], key_w),
+        (w_value.at[0], value_w),
+        (w_out.at[0], out_w),
+        (ffn_gain, ffn_gain_v),
+        (final_gain, final_gain_v),
+        (dest_shard, dest_shard_v),
+        (dest_slot, dest_slot_v),
+        (w_proj, proj_w),
+    )
     loads = [
-        pltpu.make_async_copy(src, dst, load_sem.at[i])
-        for i, (src, dst) in enumerate(
-            (
-                (w_query.at[0], query_w),
-                (w_key.at[0], key_w),
-                (w_value.at[0], value_w),
-                (w_out.at[0], out_w),
-                (w_proj, proj_w),
-            )
+        pltpu.make_async_copy(src, dst, load_sem.at[i]) for i, (src, dst) in enumerate(sources)
+    ]
+    first_rows = [
+        pltpu.make_async_copy(
+            embeds.at[0, :, pl.ds(g * COLS, COLS)], attn_in.at[g], rows_sem.at[g]
         )
+        for g in range(GROUPS)
     ]
-    for load in loads:
+    for load in loads[:3]:
         load.start()
 
+    @pl.when(section == 0)
+    def _():
+        for load in first_rows:
+            load.start()
+
+    for load in loads[3:]:
+        load.start()
+    for load in loads[:2]:
+        load.wait()
+
     passage = lax.broadcasted_iota(jnp.int32, (PPM, SEQ), 0)
-    counts = jnp.sum((segments[...] == passage).astype(F32), axis=-1, keepdims=True)
-    first = jnp.sum((segments[...] < passage).astype(F32), axis=-1, keepdims=True)
+    counts = jnp.sum((segments_v[...] == passage).astype(F32), axis=-1, keepdims=True)
+    first = jnp.sum((segments_v[...] < passage).astype(F32), axis=-1, keepdims=True)
 
     def members(token):
         at = token.astype(F32)
@@ -360,23 +388,24 @@
         ahead = k - i
         distance = jnp.abs(ahead)
         for head in range(HEADS):
-            before = jnp.broadcast_to(rel_table[0:1, head : head + 1], (ROWS, SEQ))
-            after = jnp.broadcast_to(rel_table[16:17, head : head + 1], (ROWS, SEQ))
+            before = jnp.broadcast_to(rel_v[head : head + 1, 0:1], (ROWS, SEQ))
+            after = jnp.broadcast_to(rel_v[head : head + 1, 16:17], (ROWS, SEQ))
             for code in range(1, 16):
                 reached = distance >= lowest[code]
-                before = jnp.where(reached, rel_table[code : code + 1, head : head + 1], before)
+                before = jnp.where(reached, rel_v[head : head + 1, code : code + 1], before)
                 after = jnp.where(
-                    reached, rel_table[16 + code : 17 + code, head : head + 1], after
+                    reached, rel_v[head : head + 1, 16 + code : 17 + code], after
                 )
             value = jnp.where(ahead > 0, after, before)
             bias[head, rows, :] = jnp.where(inside, value, -1e30)
 
     @pl.when(section == 0)
     def _():
-        for g in range(GROUPS):
-            attn_in[g] = embeds[0, :, g * COLS : (g + 1) * COLS]
-
-    pl.semaphore_wait(barrier, RINGZ - 1 + SHARDS - 1 + SHARDS + 2)
+        for load in first_rows:
+            load.wait()
+
+    loads[2].wait()
+    pl.semaphore_wait(barrier, RINGZ - 1 + RINGZ + SHARDS - 1)
 
     swaps = [
         copy_to(src, dst, swap_send.at[i], swap_recv.at[i], {"section": other})
@@ -399,8 +428,9 @@
     hand = copy_to(handed, ffn_in, hand_send.at[0], hand_recv.at[0], {"section": other})
 
     def near(g):
+        at = 0 if isinstance(g, pl.Slice) else g
         return copy_to(
-            staged.at[g], ffn_rows.at[g, 0], near_send.at[g], near_recv.at[g], {"section": other}
+            staged.at[g], ffn_rows.at[g, 0], near_send.at[0], near_recv.at[at], {"section": other}
         )
 
     def squares(value):
@@ -458,8 +488,9 @@
 
         return lax.fori_loop(0, GROUPS, add, no_squares)
 
-    def half(place):
-        return pl.ds(place * 4, 4), slice(place * MID, (place + 1) * MID)
+    def part(place):
+        blocks = (0, NEAR) if place == 0 else (NEAR, RINGZ - NEAR)
+        return pl.ds(*blocks), pl.ds(blocks[0] * ROWS, blocks[1] * ROWS), blocks[1] * ROWS
 
     def attention():
         total = lax.fori_loop(
@@ -469,21 +500,21 @@
 
         @pl.loop(0, GROUPS)
         def _(g):
-            value = attn_in[g].astype(F32) * scale * attn_gain[:, group_cols(g)]
+            value = attn_in[g].astype(F32) * scale * attn_gain_v[:, group_cols(g)]
             attn_rows[g, 0] = value.astype(BF16)
             attn_spread.step(1, g)
 
-        for load in loads[:3]:
+        for load in loads[3:6]:
             load.wait()
 
         def multiply(pair, place):
-            blocks, rows = half(place)
+            blocks, rows, count = part(place)
             for n, weight in enumerate((query_w, key_w, value_w)):
                 cols = slice(n * 256, (n + 1) * 256)
                 product = jnp.where(pair == 0, 0.0, sums[rows, cols])
                 for g in (2 * pair, 2 * pair + 1):
                     product = product + jnp.dot(
-                        attn_rows[g, blocks].reshape(MID, COLS),
+                        attn_rows[g, blocks].reshape(count, COLS),
                         weight[group_cols(g), :],
                         preferred_element_type=F32,
                     )
@@ -504,8 +535,8 @@
         values[...] = sums[:, 512:768].astype(BF16)
 
         def attend(place):
-            _, rows = half(place)
-            head_lane = lax.broadcasted_iota(jnp.int32, (MID, 128), 1)
+            _, rows, count = part(place)
+            head_lane = lax.broadcasted_iota(jnp.int32, (count, 128), 1)
 
             @pl.loop(0, HEADS // 2)
             def _(pair):
@@ -527,22 +558,25 @@
                 context[rows, cols] = jnp.where(head_lane < 64, results[0], results[1]).astype(BF16)
 
         def project(g, place):
-            blocks, rows = half(place)
+            blocks, rows, count = part(place)
             product = jnp.dot(
                 context[rows, :], out_w[:, group_cols(g)], preferred_element_type=F32
             )
-            attn_parts[g, blocks] = product.astype(BF16).reshape(4, ROWS, COLS)
+            attn_parts[g, blocks] = product.astype(BF16).reshape(
+                count // ROWS, ROWS, COLS
+            )
 
         attend(1)
-        loads[3].wait()
+        loads[6].wait()
         run_chains(
             attn_chains, lambda g: project(g, 1), lambda: attend(0), lambda g: project(g, 0)
         )
+        loads[7].wait()
         scale = scale_of(finish(attn_chains, attn_in, handed))
 
         @pl.loop(0, GROUPS)
         def _(g):
-            value = handed[g].astype(F32) * scale * ffn_gain[:, group_cols(g)]
+            value = handed[g].astype(F32) * scale * ffn_gain_v[:, group_cols(g)]
             staged[g] = value.astype(BF16)
             for way in (0, 1):
                 ffn_spread.move(way, 1, g, staged.at[g], other).start()
@@ -552,20 +586,20 @@
 
     def feed():
         def multiply(pair, place):
-            blocks, rows = half(place)
+            blocks, rows, count = part(place)
             for n, weight in enumerate((gate_w, up_w)):
                 cols = slice(n * HID, (n + 1) * HID)
                 product = jnp.where(pair == 0, 0.0, sums[rows, cols])
                 for j in range(2):
                     product = product + jnp.dot(
-                        ffn_rows[2 * pair + j, blocks].reshape(MID, COLS),
+                        ffn_rows[2 * pair + j, blocks].reshape(count, COLS),
                         weight[pair, 2 * j : 2 * j + 2].reshape(COLS, HID),
                         preferred_element_type=F32,
                     )
                 sums[rows, cols] = product
 
         def activate(place):
-            _, rows = half(place)
+            _, rows, count = part(place)
             gate = sums[rows, 0:HID]
             curve = jnp.tanh(0.7978845608 * (gate + 0.044715 * gate * gate * gate))
             hidden[rows, :] = (0.5 * gate * (1.0 + curve) * sums[rows, HID : 2 * HID]).astype(BF16)
@@ -596,7 +630,7 @@
         weights.land((2, 3))
 
         def project(g, place):
-            blocks, rows = half(place)
+            blocks, rows, count = part(place)
             for j in range(2):
                 product = jnp.dot(
                     hidden[rows, :],
@@ -604,7 +638,7 @@
                     preferred_element_type=F32,
                 )
                 ffn_parts[g, blocks, :, j * DK : (j + 1) * DK] = product.astype(BF16).reshape(
-                    4, ROWS, DK
+                    count // ROWS, ROWS, DK
                 )
 
         run_chains(ffn_chains, lambda g: project(g, 1), lambda: None, lambda g: project(g, 0))
@@ -641,7 +675,33 @@
         def _():
             feed()
 
-    loads[4].wait()
+    def leave():
+        for swap in swaps:
+            swap.wait_send()
+        weights.sent()
+        hand.wait_send()
+        near(pl.ds(0, GROUPS)).wait_send()
+        attn_spread.sent()
+        ffn_spread.sent(staged)
+        attn_chains.sent()
+        ffn_chains.sent()
+
+    for load in loads[8:]:
+        load.wait()
+
+    def pool_copy(k):
+        to = lax.rem(z + k, RINGZ)
+        return copy_to(
+            pooled.at[to], pooled_in.at[z], pool_send.at[k], pool_recv.at[k], {"tensor": to}
+        )
+
+    def share_copy(k, there):
+        device = {"tensor": lax.rem(z + k, RINGZ)}
+        at = k
+        if there:
+            device["section"] = other
+            at = RINGZ + k
+        return copy_to(shares.at[z], shares.at[z], share_send.at[at], share_recv.at[k], device)
 
     @pl.when(section == 0)
     def _():
@@ -650,20 +710,8 @@
         )
         scale = scale_of(total)
 
-        def pool_copy(k):
-            to = lax.rem(z + k, RINGZ)
-            return copy_to(
-                pooled.at[to], pooled_in.at[z], pool_send.at[k], pool_recv.at[k], {"tensor": to}
-            )
-
-        def share_copy(k):
-            to = lax.rem(z + k, RINGZ)
-            return copy_to(
-                shares.at[z], shares.at[z], share_send.at[k], share_recv.at[k], {"tensor": to}
-            )
-
         def pool(g):
-            finished = attn_in[g].astype(F32) * scale * final_gain[:, group_cols(g)]
+            finished = attn_in[g].astype(F32) * scale * final_gain_v[:, group_cols(g)]
             return jnp.dot(
                 member_here[...], finished, precision=HIGHEST, preferred_element_type=F32
             )
@@ -673,95 +721,63 @@
             pooled[to] = pool(to)
             pool_copy(k).start()
         pooled_in[z] = pool(z)
+        leave()
         for k in range(1, RINGZ):
             pool_copy(k).wait_recv()
         means = (jnp.sum(pooled_in[...], axis=0) / counts).astype(BF16)
         shares[z] = jnp.dot(means, proj_w[...], preferred_element_type=F32)
         for k in (4, 3, 5, 2, 6, 1, 7):
-            share_copy(k).start()
-        row = lax.broadcasted_iota(jnp.int32, (2 * SHARDS * 8, PPM), 0)
-        chosen = (dest_shard[...] == (row >> 3)) & (dest_slot[...] == (row & 3))
-        chosen = chosen.astype(F32)
-        for k in range(1, RINGZ):
-            share_copy(k).wait_recv()
-        projected = shares[0]
-        for d in range(1, RINGZ):
-            projected = projected + shares[d]
-        mean_square = jnp.mean(projected * projected, axis=-1, keepdims=True)
-        unit = (projected * lax.rsqrt(mean_square + EPS)).astype(BF16).astype(F32)
-        lower = jnp.dot(chosen, unit[:, :HALF], preferred_element_type=F32)
-        upper = jnp.dot(chosen, unit[:, HALF:], preferred_element_type=F32)
-        row = lax.broadcasted_iota(jnp.int32, (2 * SHARDS * 8, HALF), 0)
-        blocks = jnp.where((row & 7) < 4, lower, upper)
-        placed[...] = blocks.reshape(2 * SHARDS, 8, HALF)
-        placed_in[shard] = placed[shard]
-
-        @pl.loop(1, SHARDS)
-        def _(k):
-            to = lax.rem(shard + k, SHARDS)
-            copy_to(
-                placed.at[to], placed_in.at[shard], place_send.at[k], place_recv.at[k], {"shard": to}
-            ).start()
-
-        @pl.loop(0, SHARDS)
-        def _(k):
-            to = lax.rem(shard + k, SHARDS)
-            copy_to(
-                placed.at[SHARDS + to],
-                placed_in.at[shard],
-                place_send.at[SHARDS + k],
-                place_recv.at[k],
-                {"section": other, "shard": to},
-            ).start()
-
-    for swap in swaps:
-        swap.wait_send()
-    weights.sent()
-    hand.wait_send()
-
-    @pl.loop(0, GROUPS)
-    def _(g):
-        attn_spread.sent(g, (1, 2, 3, 4))
-        for way in (0, 1):
-            ffn_spread.move(way, 1, g, staged.at[g], other).wait_send()
-        ffn_spread.sent(g, (2, 3, 4))
-        near(g).wait_send()
-        attn_chains.sent(g)
-        ffn_chains.sent(g)
-
-    def place_wait(k):
+            share_copy(k, False).start()
+            share_copy(k, True).start()
+        share_copy(0, True).start()
+
+    @pl.when(section == 1)
+    def _():
+        leave()
+        share_copy(0, True).wait_recv()
+
+    row = lax.broadcasted_iota(jnp.int32, (SHARDS * 8, PPM), 0)
+    chosen = (dest_shard_v[...] == (row >> 3) + section * SHARDS) & (dest_slot_v[...] == (row & 3))
+    chosen = chosen.astype(F32)
+    for k in range(1, RINGZ):
+        share_copy(k, False).wait_recv()
+    projected = shares[0]
+    for d in range(1, RINGZ):
+        projected = projected + shares[d]
+    mean_square = jnp.mean(projected * projected, axis=-1, keepdims=True)
+    unit = (projected * lax.rsqrt(mean_square + EPS)).astype(BF16).astype(F32)
+    lower = jnp.dot(chosen, unit[:, :HALF], preferred_element_type=F32)
+    upper = jnp.dot(chosen, unit[:, HALF:], preferred_element_type=F32)
+    row = lax.broadcasted_iota(jnp.int32, (SHARDS * 8, HALF), 0)
+    placed[...] = jnp.where((row & 7) < 4, lower, upper).reshape(SHARDS, 8, HALF)
+
+    def place_copy(k):
+        to = lax.rem(shard + k, SHARDS)
         return copy_to(
-            placed.at[0], placed_in.at[0], place_send.at[k], place_recv.at[k], {"shard": shard}
+            placed.at[to], placed_in.at[shard], place_send.at[k], place_recv.at[k], {"shard": to}
         )
+
+    @pl.loop(1, SHARDS)
+    def _(k):
+        place_copy(k).start()
+
+    placed_in[shard] = placed[shard]
 
     @pl.when(section == 0)
     def _():
         for k in range(1, RINGZ):
-            pool_wait = copy_to(
-                pooled.at[0], pooled_in.at[0], pool_send.at[k], pool_recv.at[k], {"tensor": z}
-            )
-            pool_wait.wait_send()
-            share_wait = copy_to(
-                shares.at[0], shares.at[0], share_send.at[k], share_recv.at[k], {"tensor": z}
-            )
-            share_wait.wait_send()
-
-        @pl.loop(1, SHARDS)
-        def _(k):
-            place_wait(k).wait_recv()
-            place_wait(k).wait_send()
-
-        @pl.loop(SHARDS, 2 * SHARDS)
-        def _(k):
-            copy_to(
-                placed.at[0], placed_in.at[0], place_send.at[k], place_recv.at[0], {"shard": shard}
-            ).wait_send()
-
-    @pl.when(section == 1)
-    def _():
-        @pl.loop(0, SHARDS)
-        def _(k):
-            place_wait(k).wait_recv()
+            pool_copy(k).wait_send()
+            share_copy(k, False).wait_send()
+        for k in range(RINGZ):
+            share_copy(k, True).wait_send()
+
+    @pl.loop(1, SHARDS)
+    def _(k):
+        place_copy(k).wait_send()
+
+    @pl.loop(1, SHARDS)
+    def _(k):
+        place_copy(k).wait_recv()
 
     rows = jnp.sum(placed_in[...], axis=0)
     index[:, 0:HALF] = rows[0:4].astype(BF16)
@@ -794,6 +810,13 @@
     own = pltpu.VMEM((GROUPS, ROWS, COLS), BF16)
     heads = pltpu.VMEM((SEQ, 256), BF16)
     scratch = [
+        pltpu.VMEM((1, SEQ), jnp.int32),
+        pltpu.VMEM((HEADS, 32), F32),
+        pltpu.VMEM((1, WIDTH), F32),
+        pltpu.VMEM((1, WIDTH), F32),
+        pltpu.VMEM((1, WIDTH), F32),
+        pltpu.VMEM((1, PPM), jnp.int32),
+        pltpu.VMEM((1, PPM), jnp.int32),
         pltpu.VMEM((WIDTH, 256), BF16),
         pltpu.VMEM((WIDTH, 256), BF16),
         pltpu.VMEM((WIDTH, 256), BF16),
@@ -823,34 +846,34 @@
         pltpu.VMEM((RINGZ, PPM, COLS), F32),
         pltpu.VMEM((RINGZ, PPM, COLS), F32),
         pltpu.VMEM((RINGZ, PPM, EMB), F32),
-        pltpu.VMEM((2 * SHARDS, 8, HALF), F32),
         pltpu.VMEM((SHARDS, 8, HALF), F32),
-        dma((5,)),
+        pltpu.VMEM((SHARDS, 8, HALF), F32),
+        dma((12,)),
+        dma((GROUPS,)),
         dma((3,)),
         dma((3,)),
         dma((1,)),
         dma((1,)),
+        dma((1,)),
         dma((GROUPS,)),
-        dma((GROUPS,)),
+        dma((2, 8)),
         dma((2, 8, GROUPS)),
-        dma((2, 8, GROUPS)),
-        dma((2, 16, GROUPS)),
+        dma((2, 16)),
         dma((2, 16, GROUPS)),
         dma((4, 20)),
         dma((4, 20)),
         dma((RINGZ,)),
         dma((RINGZ,)),
+        dma((2 * RINGZ,)),
         dma((RINGZ,)),
-        dma((RINGZ,)),
-        dma((2 * SHARDS,)),
+        dma((SHARDS,)),
         dma((SHARDS,)),
         pltpu.SemaphoreType.REGULAR,
     ]
-    vmem_args = (0, 1, 2, 3, 8, 12, 14, 15)
     return pl.pallas_call(
         kernel,
         out_shape=jax.ShapeDtypeStruct((4, EMB), BF16),
-        in_specs=[vmem if i in vmem_args else anywhere for i in range(16)],
+        in_specs=[anywhere] * 16,
         out_specs=vmem,
         scratch_shapes=scratch,
         compiler_params=pltpu.CompilerParams(
@@ -859,7 +882,7 @@
     )(
         embeds,
         segments,
-        rel_table,
+        rel_table.T,
         attn_gain,
         w_query,
         w_key,

time: 176 us -> 172 us (0.977)
  Pallas kernels: 173 us -> 171 us
    pallas_call x1, Pallas kernels: 173 us -> 171 us  [on_device(): pl.pallas_call(kernel, out_shape=jax.ShapeDtypeStruct((4, EMB), BF16), in...]
where the time goes in v3:
time: 172 us
  Pallas kernels  171 us (99%)
    pallas_call x1, Pallas kernels, on_device(): pl.pallas_call(kernel, out_shape=jax.ShapeDtypeStruct((4, EMB), BF16), in...  171 us

profile of v3, /device:TPU:1, one launch (start us, length us, event | category | flops | bytes accessed | tf_op | source)
XLA Modules:
  0.0 172.2 jit_solution(16717337709110223480)
XLA Ops:
  0.0 170.9 %shard_map.154 = bf16[4,768]{1,0:T(4,128)(2,1)} custom-call(bf16[1,32,4096]{2,1,0:T(8,128)(2,1)} %embeds.1, s32[1,256]{1,0:T(1,128)} %segments.1, f32[4,32]{1,0:T(4,128)} %bitcast.3, f32[1,4096]{1,0:T(1,128)} %attn_gain.1, bf16[1,4096,256]{2,1,0:T(8,128)(2,1)} %w_query.1, bf16[1,4096,256]{2,1,0:T(8,128)(2,1)} %w_key.1, bf16[1,4096,256]{2,1,0:T(8,128)(2,1)} %w_value.1, ...), custom_call_target="tpu_custom_call" | custom-call | tf_op jit(solution)/shard_map/pallas_call | solution.py:873
  170.9 1.3 copy.18

commit v4 on v3

--- a/solution.py
+++ b/solution.py
@@ -18,6 +18,7 @@
 WIDTH = 4096
 GROUPS = 8
 COLS = WIDTH // GROUPS
+PAIRS = GROUPS // 2
 SEQ = 256
 NEAR = 5
 HEADS = 4
@@ -57,38 +58,46 @@
         self.beside = (lax.rem(z + 1, RINGZ), lax.rem(z + RINGZ - 1, RINGZ))
         self.rows, self.send, self.recv = rows, send, recv
 
-    def move(self, way, hop, g, src=None, section=None):
+    def move(self, way, hop, far, q, src=None, section=None):
         source, target = (RINGZ - hop + 1, RINGZ - hop) if way == 0 else (hop - 1, hop)
-        rows = pl.ds(0, ROWS) if hop < 4 else part_rows(way)
+        rows = part_rows(way if far else 1 - way)
+        groups = pl.ds(0, GROUPS) if q is None else pl.ds(2 * q, 2)
         if src is None:
-            src = self.rows.at[g, PLACE[source % RINGZ], rows]
+            src = self.rows.at[groups, PLACE[source % RINGZ], rows]
+        else:
+            src = src.at[groups, rows]
         device = {"tensor": self.beside[way]}
         if section is not None:
             device["section"] = section
-        at = way * 4 + hop - 1
+        if hop < 3 or (hop == 3 and far):
+            at = (hop - 1) * 8 + (0 if far else 4) + (0 if q is None else q)
+        else:
+            at = 20 if hop == 3 else 21
         return copy_to(
             src,
-            self.rows.at[g, PLACE[target % RINGZ], rows],
-            self.send.at[at],
-            self.recv.at[at, 0 if isinstance(g, pl.Slice) else g],
+            self.rows.at[groups, PLACE[target % RINGZ], rows],
+            self.send.at[way, 2 * hop - (2 if far else 1)],
+            self.recv.at[way, at],
             device,
         )
 
-    def step(self, hop, g):
+    def step(self, hop, far, q):
         for way in (0, 1):
             if hop > 1:
-                self.move(way, hop - 1, g).wait_recv()
-            self.move(way, hop, g).start()
-
-    def land(self, g):
+                self.move(way, hop - 1, far, q).wait_recv()
+            self.move(way, hop, far, q).start()
+
+    def land(self):
         for way in (0, 1):
-            self.move(way, 4, g).wait_recv()
+            self.move(way, 3, False, None).wait_recv()
+        for way in (0, 1):
+            self.move(way, 4, True, None).wait_recv()
 
     def sent(self, src=None):
         for way in (0, 1):
             for hop in (1, 2, 3, 4):
-                whole = pl.ds(0, GROUPS)
-                self.move(way, hop, whole, src if hop == 1 else None).wait_send()
+                for far in (True, False)[: 2 if hop < 4 else 1]:
+                    self.move(way, hop, far, None, src if hop == 1 else None).wait_send()
 
 
 class Chains:
@@ -96,46 +105,45 @@
         self.beside = (lax.rem(z + 1, RINGZ), lax.rem(z + RINGZ - 1, RINGZ))
         self.parts, self.landed, self.send, self.recv = parts, landed, send, recv
 
-    def move(self, way, hop, g, half):
-        ahead = 5 - hop
-        place = PLACE[ahead if way == 0 else RINGZ - ahead]
-        at = way * 8 + (hop - 1) * 2 + half
-        rows = part_rows(half)
+    def place(self, way, hop):
+        return PLACE[5 - hop if way == 0 else RINGZ - 5 + hop]
+
+    def move(self, way, hop, far, q):
+        rows = part_rows(way if far else 1 - way)
+        groups = pl.ds(0, GROUPS) if q is None else pl.ds(2 * q, 2)
+        kind = 2 * hop - (2 if far else 1)
+        kind = kind - 1 if hop > 1 else kind
+        at = kind * 4 + (0 if q is None or kind == 6 else q)
         return copy_to(
-            self.parts.at[g, place, rows],
-            self.landed.at[way, hop - 1, g, rows],
-            self.send.at[at],
-            self.recv.at[at, 0 if isinstance(g, pl.Slice) else g],
+            self.parts.at[groups, self.place(way, hop), rows],
+            self.landed.at[way, hop - 1, groups, rows],
+            self.send.at[way, kind],
+            self.recv.at[way, at],
             {"tensor": self.beside[way]},
         )
 
-    def forward(self, hop, g, late):
+    def forward(self, hop, far, q):
         for way in (0, 1):
-            half = way if late else 1 - way
-            if hop > (1 if late else 2):
-                self.move(way, hop - 1, g, half).wait_recv()
-                place = PLACE[5 - hop if way == 0 else RINGZ - 5 + hop]
-                rows = part_rows(half)
-                total = self.parts[g, place, rows].astype(F32) + self.landed[
-                    way, hop - 2, g, rows
+            if hop > (1 if far else 2):
+                self.move(way, hop - 1, far, q).wait_recv()
+                place = self.place(way, hop)
+                rows = part_rows(way if far else 1 - way)
+                groups = pl.ds(2 * q, 2)
+                total = self.parts[groups, place, rows].astype(F32) + self.landed[
+                    way, hop - 2, groups, rows
                 ].astype(F32)
-                self.parts[g, place, rows] = total.astype(BF16)
-            self.move(way, hop, g, half).start()
+                self.parts[groups, place, rows] = total.astype(BF16)
+            self.move(way, hop, far, q).start()
 
     def total(self, g):
-        for way in (0, 1):
-            for half in (0, 1):
-                self.move(way, 4, g, half).wait_recv()
         own = self.parts[g, 0].astype(F32)
         return own + self.landed[0, 3, g].astype(F32) + self.landed[1, 3, g].astype(F32)
 
     def sent(self):
-        whole = pl.ds(0, GROUPS)
         for way in (0, 1):
-            self.move(way, 1, whole, way).wait_send()
-            for hop in (2, 3, 4):
-                for half in (0, 1):
-                    self.move(way, hop, whole, half).wait_send()
+            for hop in (1, 2, 3, 4):
+                for far in (True, False)[: 2 if hop > 1 else 1]:
+                    self.move(way, hop, far, None).wait_send()
 
 
 class Weights:
@@ -153,22 +161,40 @@
         at_x, at_y = lax.rem(self.x + along_x, SIDE), lax.rem(self.y + along_y, SIDE)
         return ref.at[at_y, at_x, pl.ds(start, size)]
 
+    def all_of(self, array, stage, hop):
+        ref, start, size = self.arrays[array]
+        rows = pl.ds(start, size if hop == 0 else size // 2)
+        ref = ref.at[0, pl.ds(0, 2), rows] if stage == 0 else ref.at[pl.ds(0, 2), :, rows]
+        return copy_to(
+            ref,
+            ref,
+            self.send.at[array, stage * 2 + hop],
+            self.recv.at[array, 2 if stage == 0 else 11],
+            {"shard": self.y * SIDE + self.x},
+        )
+
     def copy(self, array, stage, hop, line, sign, landing):
         step = 1 if sign == 0 else SIDE - 1
         back = SIDE - step
         away = (back if hop == 1 else 0) + (back if landing else 0)
         if stage == 0:
             ref = self.piece(array, away % SIDE, 0, None if hop == 0 else sign)
-            at = hop * 2 + sign
+            at = sign if hop == 0 else 2
         else:
             ref = self.piece(array, line, away % SIDE, None if hop == 0 else sign)
-            at = 4 + (line * 2 + hop) * 2 + sign
+            at = 3 + line * 2 + sign if hop == 0 else 11
         on_x = (array % 2 == 0) == (stage == 0)
         if on_x:
             shard = self.y * SIDE + lax.rem(self.x + step, SIDE)
         else:
             shard = lax.rem(self.y + step, SIDE) * SIDE + self.x
-        return copy_to(ref, ref, self.send.at[array, at], self.recv.at[array, at], {"shard": shard})
+        return copy_to(
+            ref,
+            ref,
+            self.send.at[array, stage * 2 + hop],
+            self.recv.at[array, at],
+            {"shard": shard},
+        )
 
     def go(self, array, stage, hop, line, sign):
         self.copy(array, stage, hop, line, sign, False).start()
@@ -191,8 +217,7 @@
                 for other in both:
                     self.go(array, 1, 0, line, other)
         for array in range(4):
-            for sign in both:
-                self.wait(array, 0, 1, 0, sign)
+            self.all_of(array, 0, 1).wait_recv()
             for sign in both:
                 self.go(array, 1, 0, 2, sign)
         for array in range(4):
@@ -203,17 +228,13 @@
 
     def land(self, arrays):
         for array in arrays:
-            for line in range(SIDE):
-                for sign in (0, 1):
-                    self.wait(array, 1, 1, line, sign)
+            self.all_of(array, 1, 1).wait_recv()
 
     def sent(self):
         for array in range(4):
-            for sign in (0, 1):
+            for stage in (0, 1):
                 for hop in (0, 1):
-                    self.copy(array, 0, hop, 0, sign, False).wait_send()
-                    for line in range(SIDE):
-                        self.copy(array, 1, hop, line, sign, False).wait_send()
+                    self.all_of(array, stage, hop).wait_send()
 
 
 def kernel(
@@ -270,6 +291,8 @@
     pooled,
     pooled_in,
     shares,
+    units,
+    row_squares,
     placed,
     placed_in,
     load_sem,
@@ -290,6 +313,8 @@
     pool_recv,
     share_send,
     share_recv,
+    unit_send,
+    unit_recv,
     place_send,
     place_recv,
     free_sem,
@@ -309,8 +334,7 @@
     def _(k):
         greet({"tensor": lax.rem(z + k, RINGZ)})
 
-    @pl.loop(0, RINGZ)
-    def _(k):
+    for k in (0, 1, RINGZ - 1):
         greet({"section": other, "tensor": lax.rem(z + k, RINGZ)})
 
     @pl.loop(1, SHARDS)
@@ -336,7 +360,7 @@
     ]
     first_rows = [
         pltpu.make_async_copy(
-            embeds.at[0, :, pl.ds(g * COLS, COLS)], attn_in.at[g], rows_sem.at[g]
+            embeds.at[0, :, pl.ds(g * COLS, COLS)], attn_in.at[g], rows_sem.at[0]
         )
         for g in range(GROUPS)
     ]
@@ -352,6 +376,14 @@
         load.start()
     for load in loads[:2]:
         load.wait()
+
+    def squares(value):
+        return jnp.sum(value * value, axis=-1, keepdims=True)
+
+    def row_scale():
+        return lax.rsqrt(row_squares[:, 0:1] * (1.0 / WIDTH) + EPS)
+
+    no_squares = jnp.zeros((ROWS, 1), F32)
 
     passage = lax.broadcasted_iota(jnp.int32, (PPM, SEQ), 0)
     counts = jnp.sum((segments_v[...] == passage).astype(F32), axis=-1, keepdims=True)
@@ -401,11 +433,14 @@
 
     @pl.when(section == 0)
     def _():
-        for load in first_rows:
-            load.wait()
+        pltpu.make_async_copy(attn_in, attn_in, rows_sem.at[0]).wait()
+        total = lax.fori_loop(
+            0, GROUPS, lambda g, t: t + squares(attn_in[g].astype(F32)), no_squares
+        )
+        row_squares[...] = jnp.broadcast_to(total, row_squares.shape)
 
     loads[2].wait()
-    pl.semaphore_wait(barrier, RINGZ - 1 + RINGZ + SHARDS - 1)
+    pl.semaphore_wait(barrier, RINGZ - 1 + 3 + SHARDS - 1)
 
     swaps = [
         copy_to(src, dst, swap_send.at[i], swap_recv.at[i], {"section": other})
@@ -427,82 +462,78 @@
     weights = Weights(y, x, gate_w, up_w, down_w, w_send, w_recv)
     hand = copy_to(handed, ffn_in, hand_send.at[0], hand_recv.at[0], {"section": other})
 
-    def near(g):
-        at = 0 if isinstance(g, pl.Slice) else g
-        return copy_to(
-            staged.at[g], ffn_rows.at[g, 0], near_send.at[0], near_recv.at[at], {"section": other}
-        )
-
-    def squares(value):
-        return jnp.sum(value * value, axis=-1, keepdims=True)
-
-    def scale_of(total):
-        return lax.rsqrt(total * (1.0 / WIDTH) + EPS)
-
-    no_squares = jnp.zeros((ROWS, 1), F32)
+    near = copy_to(
+        staged, ffn_rows.at[:, 0], near_send.at[0], near_recv.at[0], {"section": other}
+    )
 
     def run_spread(spread, multiply):
-        @pl.loop(0, GROUPS)
-        def _(g):
-            spread.step(2, g)
-
-        @pl.loop(0, GROUPS)
-        def _(g):
-            spread.step(3, g)
-
-        @pl.loop(0, GROUPS // 2)
-        def _(pair):
-            multiply(pair, 0)
-            for g in (2 * pair, 2 * pair + 1):
-                spread.step(4, g)
+        for hop in (2, 3):
+            for far in (True, False):
+
+                @pl.loop(0, PAIRS)
+                def _(q):
+                    spread.step(hop, far, q)
+
+        @pl.loop(0, PAIRS)
+        def _(q):
+            multiply(q, 0)
+            spread.step(4, True, q)
 
     def run_chains(chains, far, between, close):
-        @pl.loop(0, GROUPS)
-        def _(g):
-            far(g)
-            chains.forward(1, g, True)
-            chains.forward(2, g, False)
+        @pl.loop(0, PAIRS)
+        def _(q):
+            far(2 * q)
+            far(2 * q + 1)
+            chains.forward(1, True, q)
+            chains.forward(2, False, q)
 
         between()
 
-        @pl.loop(0, GROUPS)
-        def _(g):
-            close(g)
-            chains.forward(2, g, True)
-            chains.forward(3, g, False)
-
-        @pl.loop(0, GROUPS)
-        def _(g):
-            chains.forward(3, g, True)
-            chains.forward(4, g, False)
-
-        @pl.loop(0, GROUPS)
-        def _(g):
-            chains.forward(4, g, True)
+        @pl.loop(0, PAIRS)
+        def _(q):
+            close(2 * q)
+            close(2 * q + 1)
+            chains.forward(2, True, q)
+
+        for hop, is_far in ((3, False), (3, True), (4, False), (4, True)):
+
+            @pl.loop(0, PAIRS)
+            def _(q):
+                chains.forward(hop, is_far, q)
 
     def finish(chains, before, after):
-        def add(g, total):
-            value = (before[g].astype(F32) + chains.total(g)).astype(BF16)
-            after[g] = value
-            return total + squares(value.astype(F32))
-
-        return lax.fori_loop(0, GROUPS, add, no_squares)
+        for way in (0, 1):
+            chains.move(way, 4, False, None).wait_recv()
+
+        def add(q, total):
+            for way in (0, 1):
+                chains.move(way, 4, True, q).wait_recv()
+            for g in (2 * q, 2 * q + 1):
+                value = (before[g].astype(F32) + chains.total(g)).astype(BF16)
+                after[g] = value
+                total = total + squares(value.astype(F32))
+            return total
+
+        total = lax.fori_loop(0, PAIRS, add, no_squares)
+        row_squares[...] = jnp.broadcast_to(total, row_squares.shape)
 
     def part(place):
         blocks = (0, NEAR) if place == 0 else (NEAR, RINGZ - NEAR)
         return pl.ds(*blocks), pl.ds(blocks[0] * ROWS, blocks[1] * ROWS), blocks[1] * ROWS
 
     def attention():
-        total = lax.fori_loop(
-            0, GROUPS, lambda g, t: t + squares(attn_in[g].astype(F32)), no_squares
-        )
-        scale = scale_of(total)
-
-        @pl.loop(0, GROUPS)
-        def _(g):
-            value = attn_in[g].astype(F32) * scale * attn_gain_v[:, group_cols(g)]
-            attn_rows[g, 0] = value.astype(BF16)
-            attn_spread.step(1, g)
+        scale = row_scale()
+
+        @pl.loop(0, PAIRS)
+        def _(q):
+            for g in (2 * q, 2 * q + 1):
+                value = attn_in[g].astype(F32) * scale * attn_gain_v[:, group_cols(g)]
+                attn_rows[g, 0] = value.astype(BF16)
+            attn_spread.step(1, True, q)
+
+        @pl.loop(0, PAIRS)
+        def _(q):
+            attn_spread.step(1, False, q)
 
         for load in loads[3:6]:
             load.wait()
@@ -522,9 +553,7 @@
 
         run_spread(attn_spread, multiply)
 
-        @pl.loop(0, GROUPS)
-        def _(g):
-            attn_spread.land(g)
+        attn_spread.land()
 
         @pl.loop(0, GROUPS // 2)
         def _(pair):
@@ -572,16 +601,25 @@
             attn_chains, lambda g: project(g, 1), lambda: attend(0), lambda g: project(g, 0)
         )
         loads[7].wait()
-        scale = scale_of(finish(attn_chains, attn_in, handed))
-
-        @pl.loop(0, GROUPS)
-        def _(g):
-            value = handed[g].astype(F32) * scale * ffn_gain_v[:, group_cols(g)]
-            staged[g] = value.astype(BF16)
+        finish(attn_chains, attn_in, handed)
+        scale = row_scale()
+
+        def start(far, q):
             for way in (0, 1):
-                ffn_spread.move(way, 1, g, staged.at[g], other).start()
-            near(g).start()
-
+                ffn_spread.move(way, 1, far, q, staged, other).start()
+
+        @pl.loop(0, PAIRS)
+        def _(q):
+            for g in (2 * q, 2 * q + 1):
+                value = handed[g].astype(F32) * scale * ffn_gain_v[:, group_cols(g)]
+                staged[g] = value.astype(BF16)
+            start(True, q)
+
+        @pl.loop(0, PAIRS)
+        def _(q):
+            start(False, q)
+
+        near.start()
         hand.start()
 
     def feed():
@@ -607,10 +645,7 @@
         def first_multiply(pair, place):
             @pl.when(pair == 0)
             def _():
-                @pl.loop(0, GROUPS)
-                def _(g):
-                    near(g).wait_recv()
-
+                near.wait_recv()
                 weights.land((0, 1))
 
             multiply(pair, place)
@@ -618,9 +653,7 @@
         run_spread(ffn_spread, first_multiply)
         activate(0)
 
-        @pl.loop(0, GROUPS)
-        def _(g):
-            ffn_spread.land(g)
+        ffn_spread.land()
 
         @pl.loop(0, GROUPS // 2)
         def _(pair):
@@ -680,7 +713,7 @@
             swap.wait_send()
         weights.sent()
         hand.wait_send()
-        near(pl.ds(0, GROUPS)).wait_send()
+        near.wait_send()
         attn_spread.sent()
         ffn_spread.sent(staged)
         attn_chains.sent()
@@ -692,23 +725,35 @@
     def pool_copy(k):
         to = lax.rem(z + k, RINGZ)
         return copy_to(
-            pooled.at[to], pooled_in.at[z], pool_send.at[k], pool_recv.at[k], {"tensor": to}
+            pooled.at[to], pooled_in.at[z], pool_send.at[0], pool_recv.at[0], {"tensor": to}
         )
 
-    def share_copy(k, there):
+    def share_copy(k):
         device = {"tensor": lax.rem(z + k, RINGZ)}
-        at = k
-        if there:
-            device["section"] = other
-            at = RINGZ + k
-        return copy_to(shares.at[z], shares.at[z], share_send.at[at], share_recv.at[k], device)
+        return copy_to(shares.at[z], shares.at[z], share_send.at[0], share_recv.at[0], device)
+
+    def place_copy(k):
+        to = lax.rem(shard + k, SHARDS)
+        return copy_to(
+            placed.at[to], placed_in.at[shard], place_send.at[0], place_recv.at[0], {"shard": to}
+        )
+
+    others = pl.ds(0, RINGZ - 1)
+    all_pool = copy_to(
+        pooled.at[others], pooled_in.at[others], pool_send.at[0], pool_recv.at[0], {"tensor": z}
+    )
+    all_share = copy_to(
+        shares.at[others], shares.at[others], share_send.at[0], share_recv.at[0], {"tensor": z}
+    )
+    rest = pl.ds(0, SHARDS - 1)
+    all_place = copy_to(
+        placed.at[rest], placed_in.at[rest], place_send.at[0], place_recv.at[0], {"shard": shard}
+    )
+    unit_copy = copy_to(units, units, unit_send.at[0], unit_recv.at[0], {"section": other})
 
     @pl.when(section == 0)
     def _():
-        total = lax.fori_loop(
-            0, GROUPS, lambda g, t: t + squares(attn_in[g].astype(F32)), no_squares
-        )
-        scale = scale_of(total)
+        scale = row_scale()
 
         def pool(g):
             finished = attn_in[g].astype(F32) * scale * final_gain_v[:, group_cols(g)]
@@ -722,40 +767,32 @@
             pool_copy(k).start()
         pooled_in[z] = pool(z)
         leave()
-        for k in range(1, RINGZ):
-            pool_copy(k).wait_recv()
+        all_pool.wait_recv()
         means = (jnp.sum(pooled_in[...], axis=0) / counts).astype(BF16)
         shares[z] = jnp.dot(means, proj_w[...], preferred_element_type=F32)
         for k in (4, 3, 5, 2, 6, 1, 7):
-            share_copy(k, False).start()
-            share_copy(k, True).start()
-        share_copy(0, True).start()
+            share_copy(k).start()
+        all_pool.wait_send()
+        all_share.wait_recv()
+        projected = shares[0]
+        for d in range(1, RINGZ):
+            projected = projected + shares[d]
+        mean_square = jnp.mean(projected * projected, axis=-1, keepdims=True)
+        units[...] = (projected * lax.rsqrt(mean_square + EPS)).astype(BF16).astype(F32)
+        unit_copy.start()
 
     @pl.when(section == 1)
     def _():
         leave()
-        share_copy(0, True).wait_recv()
+        unit_copy.wait_recv()
 
     row = lax.broadcasted_iota(jnp.int32, (SHARDS * 8, PPM), 0)
     chosen = (dest_shard_v[...] == (row >> 3) + section * SHARDS) & (dest_slot_v[...] == (row & 3))
     chosen = chosen.astype(F32)
-    for k in range(1, RINGZ):
-        share_copy(k, False).wait_recv()
-    projected = shares[0]
-    for d in range(1, RINGZ):
-        projected = projected + shares[d]
-    mean_square = jnp.mean(projected * projected, axis=-1, keepdims=True)
-    unit = (projected * lax.rsqrt(mean_square + EPS)).astype(BF16).astype(F32)
-    lower = jnp.dot(chosen, unit[:, :HALF], preferred_element_type=F32)
-    upper = jnp.dot(chosen, unit[:, HALF:], preferred_element_type=F32)
+    lower = jnp.dot(chosen, units[:, :HALF], preferred_element_type=F32)
+    upper = jnp.dot(chosen, units[:, HALF:], preferred_element_type=F32)
     row = lax.broadcasted_iota(jnp.int32, (SHARDS * 8, HALF), 0)
     placed[...] = jnp.where((row & 7) < 4, lower, upper).reshape(SHARDS, 8, HALF)
-
-    def place_copy(k):
-        to = lax.rem(shard + k, SHARDS)
-        return copy_to(
-            placed.at[to], placed_in.at[shard], place_send.at[k], place_recv.at[k], {"shard": to}
-        )
 
     @pl.loop(1, SHARDS)
     def _(k):
@@ -765,20 +802,11 @@
 
     @pl.when(section == 0)
     def _():
-        for k in range(1, RINGZ):
-            pool_copy(k).wait_send()
-            share_copy(k, False).wait_send()
-        for k in range(RINGZ):
-            share_copy(k, True).wait_send()
-
-    @pl.loop(1, SHARDS)
-    def _(k):
-        place_copy(k).wait_send()
-
-    @pl.loop(1, SHARDS)
-    def _(k):
-        place_copy(k).wait_recv()
-
+        all_share.wait_send()
+        unit_copy.wait_send()
+
+    all_place.wait_send()
+    all_place.wait_recv()
     rows = jnp.sum(placed_in[...], axis=0)
     index[:, 0:HALF] = rows[0:4].astype(BF16)
     index[:, HALF:EMB] = rows[4:8].astype(BF16)
@@ -846,28 +874,32 @@
         pltpu.VMEM((RINGZ, PPM, COLS), F32),
         pltpu.VMEM((RINGZ, PPM, COLS), F32),
         pltpu.VMEM((RINGZ, PPM, EMB), F32),
+        pltpu.VMEM((PPM, EMB), F32),
+        pltpu.VMEM((ROWS, 128), F32),
         pltpu.VMEM((SHARDS, 8, HALF), F32),
         pltpu.VMEM((SHARDS, 8, HALF), F32),
         dma((12,)),
-        dma((GROUPS,)),
+        dma((1,)),
         dma((3,)),
         dma((3,)),
         dma((1,)),
         dma((1,)),
         dma((1,)),
-        dma((GROUPS,)),
-        dma((2, 8)),
-        dma((2, 8, GROUPS)),
-        dma((2, 16)),
-        dma((2, 16, GROUPS)),
-        dma((4, 20)),
-        dma((4, 20)),
-        dma((RINGZ,)),
-        dma((RINGZ,)),
-        dma((2 * RINGZ,)),
-        dma((RINGZ,)),
-        dma((SHARDS,)),
-        dma((SHARDS,)),
+        dma((1,)),
+        dma((2, 2, 7)),
+        dma((2, 2, 22)),
+        dma((2, 2, 7)),
+        dma((2, 2, 25)),
+        dma((4, 4)),
+        dma((4, 12)),
+        dma((1,)),
+        dma((1,)),
+        dma((1,)),
+        dma((1,)),
+        dma((1,)),
+        dma((1,)),
+        dma((1,)),
+        dma((1,)),
         pltpu.SemaphoreType.REGULAR,
     ]
     return pl.pallas_call(

time: 172 us -> 166 us (0.965)
  Pallas kernels: 171 us -> 164 us
    pallas_call x1, Pallas kernels: 171 us -> 164 us  [on_device(): pl.pallas_call(kernel, out_shape=jax.ShapeDtypeStruct((4, EMB), BF16), in...]
where the time goes in v4:
time: 166 us; the launch traced here: 165 us
  Pallas kernels  164 us (99%)
    pallas_call x1, Pallas kernels, on_device(): pl.pallas_call(kernel, out_shape=jax.ShapeDtypeStruct((4, EMB), BF16), in...  164 us

profile of v4, /device:TPU:1, one launch (start us, length us, event | category | flops | bytes accessed | tf_op | source)
XLA Modules:
  0.0 165.4 jit_solution(14493158251294826252)
XLA Ops:
  0.0 164.1 %shard_map.154 = bf16[4,768]{1,0:T(4,128)(2,1)} custom-call(bf16[1,32,4096]{2,1,0:T(8,128)(2,1)} %embeds.1, s32[1,256]{1,0:T(1,128)} %segments.1, f32[4,32]{1,0:T(4,128)} %bitcast.3, f32[1,4096]{1,0:T(1,128)} %attn_gain.1, bf16[1,4096,256]{2,1,0:T(8,128)(2,1)} %w_query.1, bf16[1,4096,256]{2,1,0:T(8,128)(2,1)} %w_key.1, bf16[1,4096,256]{2,1,0:T(8,128)(2,1)} %w_value.1, ...), custom_call_target="tpu_custom_call" | custom-call | tf_op jit(solution)/shard_map/pallas_call | solution.py:905
  164.1 1.3 copy.18

commit v5 on v4

--- a/solution.py
+++ b/solution.py
@@ -202,25 +202,35 @@
     def wait(self, array, stage, hop, line, sign):
         self.copy(array, stage, hop, line, sign, True).wait_recv()
 
+    def second(self, array, line):
+        for sign in (0, 1):
+            self.go(array, 1, 0, line, sign)
+        if array >= 2:
+            ref = self.piece(array, line, 0, None)
+            if array % 2 == 0:
+                shard = lax.rem(self.y + 2, SIDE) * SIDE + self.x
+            else:
+                shard = self.y * SIDE + lax.rem(self.x + 2, SIDE)
+            copy_to(
+                ref, ref, self.send.at[array, 3], self.recv.at[array, 11], {"shard": shard}
+            ).start()
+
     def run(self, ready):
         both = (0, 1)
         for array in range(4):
             ready(array)
             for sign in both:
                 self.go(array, 0, 0, 0, sign)
-                self.go(array, 1, 0, 0, sign)
+            self.second(array, 0)
         for array in range(4):
             for sign in both:
                 self.wait(array, 0, 0, 0, sign)
                 self.go(array, 0, 1, 0, sign)
-                line = SIDE - 1 if sign == 0 else 1
-                for other in both:
-                    self.go(array, 1, 0, line, other)
+                self.second(array, SIDE - 1 if sign == 0 else 1)
         for array in range(4):
             self.all_of(array, 0, 1).wait_recv()
-            for sign in both:
-                self.go(array, 1, 0, 2, sign)
-        for array in range(4):
+            self.second(array, 2)
+        for array in (0, 1):
             for line in (0, 1, 3, 2):
                 for sign in both:
                     self.wait(array, 1, 0, line, sign)
@@ -228,6 +238,10 @@
 
     def land(self, arrays):
         for array in arrays:
+            if array >= 2:
+                for line in range(SIDE):
+                    for sign in (0, 1):
+                        self.wait(array, 1, 0, line, sign)
             self.all_of(array, 1, 1).wait_recv()
 
     def sent(self):
@@ -278,10 +292,9 @@
     ffn_rows,
     ffn_parts,
     ffn_landed,
-    attn_in,
     handed,
-    ffn_in,
-    staged,
+    last,
+    lane_sums,
     queries,
     keys,
     values,
@@ -299,8 +312,6 @@
     rows_sem,
     swap_send,
     swap_recv,
-    hand_send,
-    hand_recv,
     near_send,
     near_recv,
     ag_send,
@@ -349,7 +360,6 @@
         (w_key.at[0], key_w),
         (w_value.at[0], value_w),
         (w_out.at[0], out_w),
-        (ffn_gain, ffn_gain_v),
         (final_gain, final_gain_v),
         (dest_shard, dest_shard_v),
         (dest_slot, dest_slot_v),
@@ -360,7 +370,7 @@
     ]
     first_rows = [
         pltpu.make_async_copy(
-            embeds.at[0, :, pl.ds(g * COLS, COLS)], attn_in.at[g], rows_sem.at[0]
+            embeds.at[0, :, pl.ds(g * COLS, COLS)], attn_rows.at[g, 0], rows_sem.at[0]
         )
         for g in range(GROUPS)
     ]
@@ -431,16 +441,21 @@
             value = jnp.where(ahead > 0, after, before)
             bias[head, rows, :] = jnp.where(inside, value, -1e30)
 
+    loads[2].wait()
+    pl.semaphore_wait(barrier, RINGZ - 1 + 3 + SHARDS - 1)
+
+    attn_spread = Spread(z, attn_rows, ag_send.at[0], ag_recv.at[0])
+    ffn_spread = Spread(z, ffn_rows, ag_send.at[1], ag_recv.at[1])
+
     @pl.when(section == 0)
     def _():
-        pltpu.make_async_copy(attn_in, attn_in, rows_sem.at[0]).wait()
-        total = lax.fori_loop(
-            0, GROUPS, lambda g, t: t + squares(attn_in[g].astype(F32)), no_squares
-        )
-        row_squares[...] = jnp.broadcast_to(total, row_squares.shape)
-
-    loads[2].wait()
-    pl.semaphore_wait(barrier, RINGZ - 1 + 3 + SHARDS - 1)
+        own_rows = attn_rows.at[:, 0]
+        pltpu.make_async_copy(own_rows, own_rows, rows_sem.at[0]).wait()
+        for far in (True, False):
+
+            @pl.loop(0, PAIRS)
+            def _(q):
+                attn_spread.step(1, far, q)
 
     swaps = [
         copy_to(src, dst, swap_send.at[i], swap_recv.at[i], {"section": other})
@@ -452,21 +467,21 @@
             )
         )
     ]
+    swaps.append(
+        copy_to(ffn_gain, ffn_gain_v, swap_send.at[3], swap_recv.at[3], {"section": other})
+    )
     for swap in swaps:
         swap.start()
 
-    attn_spread = Spread(z, attn_rows, ag_send.at[0], ag_recv.at[0])
-    ffn_spread = Spread(z, ffn_rows, ag_send.at[1], ag_recv.at[1])
     attn_chains = Chains(z, attn_parts, attn_landed, rs_send.at[0], rs_recv.at[0])
     ffn_chains = Chains(z, ffn_parts, ffn_landed, rs_send.at[1], rs_recv.at[1])
     weights = Weights(y, x, gate_w, up_w, down_w, w_send, w_recv)
-    hand = copy_to(handed, ffn_in, hand_send.at[0], hand_recv.at[0], {"section": other})
 
     near = copy_to(
-        staged, ffn_rows.at[:, 0], near_send.at[0], near_recv.at[0], {"section": other}
-    )
-
-    def run_spread(spread, multiply):
+        handed, ffn_rows.at[:, 0], near_send.at[0], near_recv.at[0], {"section": other}
+    )
+
+    def run_spread(spread, ready, multiply):
         for hop in (2, 3):
             for far in (True, False):
 
@@ -474,10 +489,36 @@
                 def _(q):
                     spread.step(hop, far, q)
 
+        ready()
+
+        @pl.loop(0, 1)
+        def _(q):
+            multiply(q, 0)
+
         @pl.loop(0, PAIRS)
         def _(q):
+            spread.step(4, True, q)
+
+        @pl.loop(1, PAIRS)
+        def _(q):
             multiply(q, 0)
-            spread.step(4, True, q)
+
+    def prepare(rows_ref, gain, pair, place):
+        blocks, rows, count = part(place)
+        total = jnp.where(pair == 0, 0.0, lane_sums[rows, :])
+        prepared = []
+        for g in (2 * pair, 2 * pair + 1):
+            value = rows_ref[g, blocks].reshape(count, COLS).astype(F32)
+            for c in range(0, COLS, 128):
+                piece = value[:, c : c + 128]
+                total = total + piece * piece
+            prepared.append((value * gain[:, group_cols(g)]).astype(BF16))
+        lane_sums[rows, :] = total
+        return prepared
+
+    def scale_of(sums_of_lanes):
+        total = jnp.sum(sums_of_lanes, axis=-1, keepdims=True)
+        return lax.rsqrt(total * (1.0 / WIDTH) + EPS)
 
     def run_chains(chains, far, between, close):
         @pl.loop(0, PAIRS)
@@ -501,17 +542,19 @@
             def _(q):
                 chains.forward(hop, is_far, q)
 
-    def finish(chains, before, after):
+    def finish(chains, before, pass_on):
         for way in (0, 1):
             chains.move(way, 4, False, None).wait_recv()
 
         def add(q, total):
             for way in (0, 1):
                 chains.move(way, 4, True, q).wait_recv()
+            ready = []
             for g in (2 * q, 2 * q + 1):
-                value = (before[g].astype(F32) + chains.total(g)).astype(BF16)
-                after[g] = value
+                value = (before[g, 0].astype(F32) + chains.total(g)).astype(BF16)
                 total = total + squares(value.astype(F32))
+                ready.append((g, value))
+            pass_on(q, ready)
             return total
 
         total = lax.fori_loop(0, PAIRS, add, no_squares)
@@ -522,46 +565,35 @@
         return pl.ds(*blocks), pl.ds(blocks[0] * ROWS, blocks[1] * ROWS), blocks[1] * ROWS
 
     def attention():
-        scale = row_scale()
-
-        @pl.loop(0, PAIRS)
-        def _(q):
-            for g in (2 * q, 2 * q + 1):
-                value = attn_in[g].astype(F32) * scale * attn_gain_v[:, group_cols(g)]
-                attn_rows[g, 0] = value.astype(BF16)
-            attn_spread.step(1, True, q)
-
-        @pl.loop(0, PAIRS)
-        def _(q):
-            attn_spread.step(1, False, q)
-
-        for load in loads[3:6]:
-            load.wait()
+        def ready():
+            for load in loads[3:6]:
+                load.wait()
 
         def multiply(pair, place):
-            blocks, rows, count = part(place)
+            prepared = prepare(attn_rows, attn_gain_v, pair, place)
+            _, rows, _ = part(place)
             for n, weight in enumerate((query_w, key_w, value_w)):
                 cols = slice(n * 256, (n + 1) * 256)
                 product = jnp.where(pair == 0, 0.0, sums[rows, cols])
-                for g in (2 * pair, 2 * pair + 1):
+                for j in range(2):
                     product = product + jnp.dot(
-                        attn_rows[g, blocks].reshape(count, COLS),
-                        weight[group_cols(g), :],
+                        prepared[j],
+                        weight[group_cols(2 * pair + j), :],
                         preferred_element_type=F32,
                     )
                 sums[rows, cols] = product
 
-        run_spread(attn_spread, multiply)
-
+        run_spread(attn_spread, ready, multiply)
         attn_spread.land()
 
-        @pl.loop(0, GROUPS // 2)
+        @pl.loop(0, PAIRS)
         def _(pair):
             multiply(pair, 1)
 
-        queries[...] = sums[:, 0:256].astype(BF16)
-        keys[...] = sums[:, 256:512].astype(BF16)
-        values[...] = sums[:, 512:768].astype(BF16)
+        scale = scale_of(lane_sums[...])
+        queries[...] = (sums[:, 0:256] * scale).astype(BF16)
+        keys[...] = (sums[:, 256:512] * scale).astype(BF16)
+        values[...] = (sums[:, 512:768] * scale).astype(BF16)
 
         def attend(place):
             _, rows, count = part(place)
@@ -600,62 +632,63 @@
         run_chains(
             attn_chains, lambda g: project(g, 1), lambda: attend(0), lambda g: project(g, 0)
         )
-        loads[7].wait()
-        finish(attn_chains, attn_in, handed)
-        scale = row_scale()
 
         def start(far, q):
             for way in (0, 1):
-                ffn_spread.move(way, 1, far, q, staged, other).start()
-
-        @pl.loop(0, PAIRS)
-        def _(q):
-            for g in (2 * q, 2 * q + 1):
-                value = handed[g].astype(F32) * scale * ffn_gain_v[:, group_cols(g)]
-                staged[g] = value.astype(BF16)
+                ffn_spread.move(way, 1, far, q, handed, other).start()
+
+        def pass_on(q, ready):
+            for g, value in ready:
+                handed[g] = value
             start(True, q)
+
+        finish(attn_chains, attn_rows, pass_on)
 
         @pl.loop(0, PAIRS)
         def _(q):
             start(False, q)
 
         near.start()
-        hand.start()
 
     def feed():
         def multiply(pair, place):
-            blocks, rows, count = part(place)
+            prepared = prepare(ffn_rows, ffn_gain_v, pair, place)
+            _, rows, _ = part(place)
             for n, weight in enumerate((gate_w, up_w)):
                 cols = slice(n * HID, (n + 1) * HID)
                 product = jnp.where(pair == 0, 0.0, sums[rows, cols])
                 for j in range(2):
                     product = product + jnp.dot(
-                        ffn_rows[2 * pair + j, blocks].reshape(count, COLS),
+                        prepared[j],
                         weight[pair, 2 * j : 2 * j + 2].reshape(COLS, HID),
                         preferred_element_type=F32,
                     )
                 sums[rows, cols] = product
 
         def activate(place):
-            _, rows, count = part(place)
-            gate = sums[rows, 0:HID]
+            _, rows, _ = part(place)
+            scale = scale_of(lane_sums[rows, :])
+            gate = sums[rows, 0:HID] * scale
+            up = sums[rows, HID : 2 * HID] * scale
             curve = jnp.tanh(0.7978845608 * (gate + 0.044715 * gate * gate * gate))
-            hidden[rows, :] = (0.5 * gate * (1.0 + curve) * sums[rows, HID : 2 * HID]).astype(BF16)
-
-        def first_multiply(pair, place):
-            @pl.when(pair == 0)
+            hidden[rows, :] = (0.5 * gate * (1.0 + curve) * up).astype(BF16)
+
+        def ready():
+            near.wait_recv()
+            swaps[3].wait_recv()
+            weights.land((0, 1))
+
+            @pl.when(section == 1)
             def _():
-                near.wait_recv()
-                weights.land((0, 1))
-
-            multiply(pair, place)
-
-        run_spread(ffn_spread, first_multiply)
+                pl.semaphore_signal(
+                    free_sem, inc=1, device_id={"section": other}, device_id_type=MESH
+                )
+
+        run_spread(ffn_spread, ready, multiply)
         activate(0)
-
         ffn_spread.land()
 
-        @pl.loop(0, GROUPS // 2)
+        @pl.loop(0, PAIRS)
         def _(pair):
             multiply(pair, 1)
 
@@ -675,8 +708,26 @@
                 )
 
         run_chains(ffn_chains, lambda g: project(g, 1), lambda: None, lambda g: project(g, 0))
-        hand.wait_recv()
-        finish(ffn_chains, ffn_in, attn_in)
+
+        def pass_on(q, ready):
+            @pl.when(section == 0)
+            def _():
+                for g, value in ready:
+                    last[g] = value
+
+            @pl.when(section == 1)
+            def _():
+                for g, value in ready:
+                    attn_rows[g, 0] = value
+                attn_spread.step(1, True, q)
+
+        finish(ffn_chains, ffn_rows, pass_on)
+
+        @pl.when(section == 1)
+        def _():
+            @pl.loop(0, PAIRS)
+            def _(q):
+                attn_spread.step(1, False, q)
 
     @pl.loop(0, 3)
     def _(turn):
@@ -698,12 +749,6 @@
 
             weights.run(ready)
 
-            @pl.when(section == 1)
-            def _():
-                pl.semaphore_signal(
-                    free_sem, inc=1, device_id={"section": other}, device_id_type=MESH
-                )
-
         @pl.when(role == 2)
         def _():
             feed()
@@ -712,14 +757,13 @@
         for swap in swaps:
             swap.wait_send()
         weights.sent()
-        hand.wait_send()
         near.wait_send()
         attn_spread.sent()
-        ffn_spread.sent(staged)
+        ffn_spread.sent(handed)
         attn_chains.sent()
         ffn_chains.sent()
 
-    for load in loads[8:]:
+    for load in loads[7:]:
         load.wait()
 
     def pool_copy(k):
@@ -756,7 +800,7 @@
         scale = row_scale()
 
         def pool(g):
-            finished = attn_in[g].astype(F32) * scale * final_gain_v[:, group_cols(g)]
+            finished = last[g].astype(F32) * scale * final_gain_v[:, group_cols(g)]
             return jnp.dot(
                 member_here[...], finished, precision=HIGHEST, preferred_element_type=F32
             )
@@ -863,8 +907,7 @@
         landed,
         own,
         own,
-        own,
-        own,
+        pltpu.VMEM((SEQ, 128), F32),
         heads,
         heads,
         heads,
@@ -878,12 +921,10 @@
         pltpu.VMEM((ROWS, 128), F32),
         pltpu.VMEM((SHARDS, 8, HALF), F32),
         pltpu.VMEM((SHARDS, 8, HALF), F32),
-        dma((12,)),
-        dma((1,)),
-        dma((3,)),
-        dma((3,)),
-        dma((1,)),
-        dma((1,)),
+        dma((11,)),
+        dma((1,)),
+        dma((4,)),
+        dma((4,)),
         dma((1,)),
         dma((1,)),
         dma((2, 2, 7)),

time: 166 us -> 163 us (0.982)
  Pallas kernels: 164 us -> 162 us
    pallas_call x1, Pallas kernels: 164 us -> 162 us  [on_device(): pl.pallas_call(kernel, out_shape=jax.ShapeDtypeStruct((4, EMB), BF16), in...]
where the time goes in v5:
time: 163 us
  Pallas kernels  162 us (99%)
    pallas_call x1, Pallas kernels, on_device(): pl.pallas_call(kernel, out_shape=jax.ShapeDtypeStruct((4, EMB), BF16), in...  162 us

profile of v5, /device:TPU:1, one launch (start us, length us, event | category | flops | bytes accessed | tf_op | source)
XLA Modules:
  0.0 162.8 jit_solution(18217556535027647345)
XLA Ops:
  0.0 161.5 %shard_map.154 = bf16[4,768]{1,0:T(4,128)(2,1)} custom-call(bf16[1,32,4096]{2,1,0:T(8,128)(2,1)} %embeds.1, s32[1,256]{1,0:T(1,128)} %segments.1, f32[4,32]{1,0:T(4,128)} %bitcast.3, f32[1,4096]{1,0:T(1,128)} %attn_gain.1, bf16[1,4096,256]{2,1,0:T(8,128)(2,1)} %w_query.1, bf16[1,4096,256]{2,1,0:T(8,128)(2,1)} %w_key.1, bf16[1,4096,256]{2,1,0:T(8,128)(2,1)} %w_value.1, ...), custom_call_target="tpu_custom_call" | custom-call | tf_op jit(solution)/shard_map/pallas_call | solution.py:946
  161.5 1.3 copy.18

commit v6 on v5

--- a/solution.py
+++ b/solution.py
@@ -202,39 +202,61 @@
     def wait(self, array, stage, hop, line, sign):
         self.copy(array, stage, hop, line, sign, True).wait_recv()
 
+    def direct(self, array, stage, line):
+        ref = self.piece(array, line, 0, None)
+        if (array % 2 == 0) == (stage == 0):
+            shard = self.y * SIDE + lax.rem(self.x + 2, SIDE)
+        else:
+            shard = lax.rem(self.y + 2, SIDE) * SIDE + self.x
+        return copy_to(
+            ref,
+            ref,
+            self.send.at[array, stage * 2 + 1],
+            self.recv.at[array, 2 if stage == 0 else 11],
+            {"shard": shard},
+        )
+
     def second(self, array, line):
         for sign in (0, 1):
             self.go(array, 1, 0, line, sign)
         if array >= 2:
-            ref = self.piece(array, line, 0, None)
-            if array % 2 == 0:
-                shard = lax.rem(self.y + 2, SIDE) * SIDE + self.x
-            else:
-                shard = self.y * SIDE + lax.rem(self.x + 2, SIDE)
-            copy_to(
-                ref, ref, self.send.at[array, 3], self.recv.at[array, 11], {"shard": shard}
-            ).start()
+            self.direct(array, 1, line).start()
 
     def run(self, ready):
-        both = (0, 1)
-        for array in range(4):
-            ready(array)
-            for sign in both:
-                self.go(array, 0, 0, 0, sign)
-            self.second(array, 0)
-        for array in range(4):
-            for sign in both:
+        def begin(arrays):
+            for array in arrays:
+                ready(array)
+                for sign in (0, 1):
+                    self.go(array, 0, 0, 0, sign)
+                if array >= 2:
+                    self.direct(array, 0, 0).start()
+                self.second(array, 0)
+
+        def along(line):
+            for array in (0, 1):
+                for sign in (0, 1):
+                    self.wait(array, 1, 0, line, sign)
+                    self.go(array, 1, 1, line, sign)
+
+        begin((0, 1))
+        for array in (0, 1):
+            for sign in (0, 1):
                 self.wait(array, 0, 0, 0, sign)
                 self.go(array, 0, 1, 0, sign)
                 self.second(array, SIDE - 1 if sign == 0 else 1)
-        for array in range(4):
+        for array in (0, 1):
             self.all_of(array, 0, 1).wait_recv()
             self.second(array, 2)
-        for array in (0, 1):
-            for line in (0, 1, 3, 2):
-                for sign in both:
-                    self.wait(array, 1, 0, line, sign)
-                    self.go(array, 1, 1, line, sign)
+        along(0)
+        begin((2, 3))
+        for line in (1, 3, 2):
+            along(line)
+        for array in (2, 3):
+            for sign in (0, 1):
+                self.wait(array, 0, 0, 0, sign)
+                self.second(array, SIDE - 1 if sign == 0 else 1)
+            self.all_of(array, 0, 1).wait_recv()
+            self.second(array, 2)
 
     def land(self, arrays):
         for array in arrays:
@@ -678,12 +700,6 @@
             swaps[3].wait_recv()
             weights.land((0, 1))
 
-            @pl.when(section == 1)
-            def _():
-                pl.semaphore_signal(
-                    free_sem, inc=1, device_id={"section": other}, device_id_type=MESH
-                )
-
         run_spread(ffn_spread, ready, multiply)
         activate(0)
         ffn_spread.land()
@@ -694,6 +710,10 @@
 
         activate(1)
         weights.land((2, 3))
+
+        @pl.when(section == 1)
+        def _():
+            pl.semaphore_signal(free_sem, inc=1, device_id={"section": other}, device_id_type=MESH)
 
         def project(g, place):
             blocks, rows, count = part(place)

time: 163 us -> 159 us (0.975)
  Pallas kernels: 162 us -> 157 us
    pallas_call x1, Pallas kernels: 162 us -> 157 us  [on_device(): pl.pallas_call(kernel, out_shape=jax.ShapeDtypeStruct((4, EMB), BF16), in...]
where the time goes in v6:
time: 159 us
  Pallas kernels  157 us (99%)
    pallas_call x1, Pallas kernels, on_device(): pl.pallas_call(kernel, out_shape=jax.ShapeDtypeStruct((4, EMB), BF16), in...  157 us

profile of v6, /device:TPU:1, one launch (start us, length us, event | category | flops | bytes accessed | tf_op | source)
XLA Modules:
  0.0 158.6 jit_solution(2305467304598718829)
XLA Ops:
  0.0 157.3 %shard_map.154 = bf16[4,768]{1,0:T(4,128)(2,1)} custom-call(bf16[1,32,4096]{2,1,0:T(8,128)(2,1)} %embeds.1, s32[1,256]{1,0:T(1,128)} %segments.1, f32[4,32]{1,0:T(4,128)} %bitcast.3, f32[1,4096]{1,0:T(1,128)} %attn_gain.1, bf16[1,4096,256]{2,1,0:T(8,128)(2,1)} %w_query.1, bf16[1,4096,256]{2,1,0:T(8,128)(2,1)} %w_key.1, bf16[1,4096,256]{2,1,0:T(8,128)(2,1)} %w_value.1, ...), custom_call_target="tpu_custom_call" | custom-call | tf_op jit(solution)/shard_map/pallas_call | solution.py:966
  157.3 1.3 copy.18

commit v7 on v6

--- a/solution.py
+++ b/solution.py
@@ -182,7 +182,7 @@
             at = sign if hop == 0 else 2
         else:
             ref = self.piece(array, line, away % SIDE, None if hop == 0 else sign)
-            at = 3 + line * 2 + sign if hop == 0 else 11
+            at = 3 + line * 2 + sign if hop == 0 and array < 2 else 11
         on_x = (array % 2 == 0) == (stage == 0)
         if on_x:
             shard = self.y * SIDE + lax.rem(self.x + step, SIDE)
@@ -260,11 +260,18 @@
 
     def land(self, arrays):
         for array in arrays:
-            if array >= 2:
-                for line in range(SIDE):
-                    for sign in (0, 1):
-                        self.wait(array, 1, 0, line, sign)
-            self.all_of(array, 1, 1).wait_recv()
+            if array < 2:
+                self.all_of(array, 1, 1).wait_recv()
+            else:
+                ref, start, size = self.arrays[array]
+                ref = ref.at[pl.ds(0, 3), :, pl.ds(start, size)]
+                copy_to(
+                    ref,
+                    ref,
+                    self.send.at[array, 2],
+                    self.recv.at[array, 11],
+                    {"shard": self.y * SIDE + self.x},
+                ).wait_recv()
 
     def sent(self):
         for array in range(4):
@@ -825,22 +832,27 @@
                 member_here[...], finished, precision=HIGHEST, preferred_element_type=F32
             )
 
+        def stacked(value):
+            cut = value.shape[1] // 2
+            return jnp.concatenate([value[:, :cut], value[:, cut:]], axis=0).astype(BF16)
+
         for k in (4, 3, 5, 2, 6, 1, 7):
             to = lax.rem(z + k, RINGZ)
-            pooled[to] = pool(to)
+            pooled[to] = stacked(pool(to))
             pool_copy(k).start()
-        pooled_in[z] = pool(z)
+        pooled_in[z] = stacked(pool(z))
         leave()
         all_pool.wait_recv()
-        means = (jnp.sum(pooled_in[...], axis=0) / counts).astype(BF16)
-        shares[z] = jnp.dot(means, proj_w[...], preferred_element_type=F32)
+        whole = jnp.sum(pooled_in[...].astype(F32), axis=0)
+        whole = jnp.concatenate([whole[:PPM], whole[PPM:]], axis=1)
+        means = (whole / counts).astype(BF16)
+        shares[z] = stacked(jnp.dot(means, proj_w[...], preferred_element_type=F32))
         for k in (4, 3, 5, 2, 6, 1, 7):
             share_copy(k).start()
         all_pool.wait_send()
         all_share.wait_recv()
-        projected = shares[0]
-        for d in range(1, RINGZ):
-            projected = projected + shares[d]
+        projected = jnp.sum(shares[...].astype(F32), axis=0)
+        projected = jnp.concatenate([projected[:PPM], projected[PPM:]], axis=1)
         mean_square = jnp.mean(projected * projected, axis=-1, keepdims=True)
         units[...] = (projected * lax.rsqrt(mean_square + EPS)).astype(BF16).astype(F32)
         unit_copy.start()
@@ -934,9 +946,9 @@
         heads,
         pltpu.VMEM((SEQ, 2 * HID), F32),
         pltpu.VMEM((SEQ, HID), BF16),
-        pltpu.VMEM((RINGZ, PPM, COLS), F32),
-        pltpu.VMEM((RINGZ, PPM, COLS), F32),
-        pltpu.VMEM((RINGZ, PPM, EMB), F32),
+        pltpu.VMEM((RINGZ, 2 * PPM, COLS // 2), BF16),
+        pltpu.VMEM((RINGZ, 2 * PPM, COLS // 2), BF16),
+        pltpu.VMEM((RINGZ, 2 * PPM, HALF), BF16),
         pltpu.VMEM((PPM, EMB), F32),
         pltpu.VMEM((ROWS, 128), F32),
         pltpu.VMEM((SHARDS, 8, HALF), F32),

time: 159 us -> 158 us (level)
  no operation moved by 1% of the time
where the time goes in v7:
time: 158 us; the launch traced here: 157 us
  Pallas kernels  156 us (99%)
    pallas_call x1, Pallas kernels, on_device(): pl.pallas_call(kernel, out_shape=jax.ShapeDtypeStruct((4, EMB), BF16), in...  156 us

profile of v7, /device:TPU:1, one launch (start us, length us, event | category | flops | bytes accessed | tf_op | source)
XLA Modules:
  0.0 157.4 jit_solution(16521456477106647613)
XLA Ops:
  0.0 156.1 %shard_map.154 = bf16[4,768]{1,0:T(4,128)(2,1)} custom-call(bf16[1,32,4096]{2,1,0:T(8,128)(2,1)} %embeds.1, s32[1,256]{1,0:T(1,128)} %segments.1, f32[4,32]{1,0:T(4,128)} %bitcast.3, f32[1,4096]{1,0:T(1,128)} %attn_gain.1, bf16[1,4096,256]{2,1,0:T(8,128)(2,1)} %w_query.1, bf16[1,4096,256]{2,1,0:T(8,128)(2,1)} %w_key.1, bf16[1,4096,256]{2,1,0:T(8,128)(2,1)} %w_value.1, ...), custom_call_target="tpu_custom_call" | custom-call | tf_op jit(solution)/shard_map/pallas_call | solution.py:978
  156.1 1.3 copy.18

commit v8 on v7

--- a/solution.py
+++ b/solution.py
@@ -474,7 +474,7 @@
     pl.semaphore_wait(barrier, RINGZ - 1 + 3 + SHARDS - 1)
 
     attn_spread = Spread(z, attn_rows, ag_send.at[0], ag_recv.at[0])
-    ffn_spread = Spread(z, ffn_rows, ag_send.at[1], ag_recv.at[1])
+    ffn_spread = Spread(z, ffn_rows, ag_send.at[1], ag_recv.at[0])
 
     @pl.when(section == 0)
     def _():
@@ -503,7 +503,7 @@
         swap.start()
 
     attn_chains = Chains(z, attn_parts, attn_landed, rs_send.at[0], rs_recv.at[0])
-    ffn_chains = Chains(z, ffn_parts, ffn_landed, rs_send.at[1], rs_recv.at[1])
+    ffn_chains = Chains(z, ffn_parts, ffn_landed, rs_send.at[1], rs_recv.at[0])
     weights = Weights(y, x, gate_w, up_w, down_w, w_send, w_recv)
 
     near = copy_to(
@@ -960,9 +960,9 @@
         dma((1,)),
         dma((1,)),
         dma((2, 2, 7)),
-        dma((2, 2, 22)),
+        dma((1, 2, 22)),
         dma((2, 2, 7)),
-        dma((2, 2, 25)),
+        dma((1, 2, 25)),
         dma((4, 4)),
         dma((4, 12)),
         dma((1,)),

time: 158 us -> 157 us (level)
  no operation moved by 1% of the time
where the time goes in v8:
time: 157 us
  Pallas kernels  155 us (99%)
    pallas_call x1, Pallas kernels, on_device(): pl.pallas_call(kernel, out_shape=jax.ShapeDtypeStruct((4, EMB), BF16), in...  155 us

profile of v8, /device:TPU:1, one launch (start us, length us, event | category | flops | bytes accessed | tf_op | source)
XLA Modules:
  0.0 156.5 jit_solution(10406609879085870485)
XLA Ops:
  0.0 155.2 %shard_map.154 = bf16[4,768]{1,0:T(4,128)(2,1)} custom-call(bf16[1,32,4096]{2,1,0:T(8,128)(2,1)} %embeds.1, s32[1,256]{1,0:T(1,128)} %segments.1, f32[4,32]{1,0:T(4,128)} %bitcast.3, f32[1,4096]{1,0:T(1,128)} %attn_gain.1, bf16[1,4096,256]{2,1,0:T(8,128)(2,1)} %w_query.1, bf16[1,4096,256]{2,1,0:T(8,128)(2,1)} %w_key.1, bf16[1,4096,256]{2,1,0:T(8,128)(2,1)} %w_value.1, ...), custom_call_target="tpu_custom_call" | custom-call | tf_op jit(solution)/shard_map/pallas_call | solution.py:978
  155.2 1.3 copy.18
